TPU v7x, 32 devices: a whole 2x2x4 slice. The times are simulated.
32 devices in a mesh: seq: 8 (over z, x), head: 4 (over y, core).
Axes of the slice: x: 2, y: 2, z: 4, core: 2. Of those that a mesh axis runs over, the one named last changes fastest.
Arguments:
- tokens: bfloat16 [8, 2048, 512], P(None, 'seq', 'head'), may hold values from -6 to 6
- norm_gain: float32 [512], replicated, may hold values from 0.5 to 1.5
- query_weight: bfloat16 [512, 512], P(None, 'head'), may hold values from -0.25 to 0.25
- key_weight: bfloat16 [512, 512], P(None, 'head'), may hold values from -0.25 to 0.25
- value_weight: bfloat16 [512, 512], P(None, 'head'), may hold values from -0.25 to 0.25
- attention_output_weight: bfloat16 [512, 512], P('head'), may hold values from -1.5 to 1.5
- feedforward_norm_gain: float32 [512], replicated, may hold values from 0.5 to 1.5
- up_weight: bfloat16 [512, 2048], P(None, 'head'), may hold values from -0.25 to 0.25
- down_weight: bfloat16 [2048, 512], P('head'), may hold values from -0.1875 to 0.1875
- segment_ids: int32 [8, 2048], P(None, 'seq'), may hold values from 0 to 15, never falling along the last dimension, each value on 1 to 1024 neighbouring positions
- out_grad: bfloat16 [8, 2048, 512], P(None, 'seq', 'head'), may hold values from -6 to 6
Outputs:
- layer_out: bfloat16 [8, 2048, 512], P(None, 'seq', 'head')
- input_grad: float32 [8, 2048, 512], P(None, 'seq', 'head')
- norm_gain_grad: float32 [512], P('head')
- query_weight_grad: float32 [512, 512], P(None, 'head')
- key_weight_grad: float32 [512, 512], P(None, 'head')
- value_weight_grad: float32 [512, 512], P(None, 'head')
- out_weight_grad: float32 [512, 512], P('head')
- ffn_gain_grad: float32 [512], P('head')
- up_weight_grad: float32 [512, 2048], P(None, 'head')
- down_weight_grad: float32 [2048, 512], P('head')
Inputs may be any that keep to these rules, and one draw needn't show every extreme that they name: `segment_ids`: in each sequence the ids start at 0 and rise by one at each document start; 16 documents of 1 to 1024 tokens, the longest exactly 1024.
All inputs are finite; a program needn't handle non-finite values.
Results may differ from a plain program's by a relative error of at most 0.017.
Values may be sent and summed in bfloat16 or wider, within the bound.
A program may use at most 256 MiB of HBM per device.

v0:
```python
import jax
import jax.numpy as jnp
from jax import lax
from jax.sharding import PartitionSpec as P

DH = 64
BLOCK = 256


FULL_PRECISION = lax.Precision.HIGHEST
EPSILON = 1e-05


def prefix(value, axis, join, neutral):
    count, mine = (lax.axis_size(axis), lax.axis_index(axis))
    pieces = jax.tree.map(lambda part: lax.all_gather(part, axis), value)
    running = jax.tree.map(
        lambda part, zero: jnp.full_like(part, 0) + jnp.asarray(zero, part.dtype), value, neutral
    )

    def prefix_lap(position, running):
        longer = join(running, jax.tree.map(lambda part: part[position], pieces))
        return jax.tree.map(lambda new, old: jnp.where(position < mine, new, old), longer, running)

    return lax.fori_loop(0, count - 1, prefix_lap, running)


def carried_in(shard, axis, combine, identity):
    count, place = (lax.axis_size(axis), lax.axis_index(axis))
    everything = jax.tree.map(
        lambda part, kind: lax.all_gather(part.astype(kind), axis),
        shard,
        (jnp.bfloat16, jnp.bfloat16, jnp.bfloat16),
    )
    start = jax.tree.map(
        lambda part, zero: jnp.broadcast_to(jnp.asarray(zero, part.dtype), part.shape),
        shard,
        identity,
    )

    def carried_lap(k, before):
        at = count - 1 - k
        reached = at > place
        new = combine(
            before, jax.tree.map(lambda part, own: part[at].astype(own.dtype), everything, shard)
        )
        return jax.tree.map(lambda a, b: jnp.where(reached, a, b), new, before)

    return lax.fori_loop(0, count, carried_lap, start)


def feature(values):
    return jnp.where(values > 0, values + 1.0, jnp.exp(jnp.minimum(values, 0.0)))


def feature_slope(values):
    return jnp.where(values > 0, 1.0, jnp.exp(jnp.minimum(values, 0.0)))


def silu_slope(values):
    sigma = jax.nn.sigmoid(values)
    return sigma * (1.0 + values * (1.0 - sigma))


def normalize(values):
    center = values - jnp.mean(values, axis=-1, keepdims=True)
    scale_inv = lax.rsqrt(jnp.mean(center * center, axis=-1, keepdims=True) + EPSILON)
    return (center * scale_inv, scale_inv)


def norm_back(grad_part, unit_rows, scale_inv, gain_row, col_share, head_index):
    full_width = unit_rows.shape[2]
    col_start = head_index * col_share
    unit_share = lax.dynamic_slice_in_dim(unit_rows, col_start, col_share, 2)
    grad_share = lax.psum_scatter(grad_part, "head", scatter_dimension=2, tiled=True)
    gain_share = lax.dynamic_slice_in_dim(gain_row, col_start, col_share, 0)
    scaled_share = grad_share * gain_share
    first_sum, second_sum = lax.psum(
        (jnp.sum(scaled_share, axis=-1), jnp.sum(scaled_share * unit_share, axis=-1)), "head"
    )
    result = scale_inv * (
        scaled_share
        - first_sum[..., None] / full_width
        - unit_share * second_sum[..., None] / full_width
    )
    gain_grad = jnp.sum(grad_share * unit_share, axis=(0, 1))
    return (result, gain_grad)


def block_terms(state_in, query_blk, key_blk, value_blk, seg_blk):
    prior_s, previous_normalizer, prior_last = state_in
    span = seg_blk.shape[1]
    causal = jnp.tril(jnp.ones((span, span), jnp.float32))
    same_mask = causal[None] * (seg_blk[:, :, None] == seg_blk[:, None, :]).astype(jnp.float32)
    scores = (
        jnp.einsum("mthd,mshd->mhts", query_blk, key_blk, preferred_element_type=jnp.float32)
        * same_mask[:, None]
    )
    scores_low = scores.astype(jnp.bfloat16)
    carry_on = (seg_blk == prior_last[:, None]).astype(jnp.float32)
    query_expanded = query_blk.astype(jnp.float32)
    numerator = jnp.einsum(
        "mhts,mshe->mthe", scores_low, value_blk, preferred_element_type=jnp.float32
    )
    numerator = numerator + carry_on[:, :, None, None] * jnp.einsum(
        "mthd,mhde->mthe", query_expanded, prior_s, precision=FULL_PRECISION
    )
    denominator = jnp.transpose(jnp.sum(scores, axis=3), (0, 2, 1))
    denominator = denominator + carry_on[:, :, None] * jnp.einsum(
        "pyqc,pqc->pyq", query_expanded, previous_normalizer, precision=FULL_PRECISION
    )
    block_last = seg_blk[:, -1]
    tail_mask = (seg_blk == block_last[:, None]).astype(jnp.float32)
    tail_keys = key_blk * tail_mask[:, :, None, None].astype(jnp.bfloat16)
    block_s = jnp.einsum(
        "mshd,mshe->mhde", tail_keys, value_blk, preferred_element_type=jnp.float32
    )
    block_z = jnp.sum(tail_keys.astype(jnp.float32), axis=1)
    keep_gate = (prior_last >= block_last).astype(jnp.float32)
    final_state = (
        block_s + keep_gate[:, None, None, None] * prior_s,
        block_z + keep_gate[:, None, None] * previous_normalizer,
        jnp.maximum(prior_last, block_last),
    )
    return (
        final_state,
        numerator,
        denominator,
        scores_low,
        same_mask,
        carry_on,
        tail_mask,
        keep_gate,
    )


def block_back(grad_state, items):
    query_blk, key_blk, value_blk, seg_blk, prior_s, previous_normalizer, prior_last, attn_blk = (
        items
    )
    grad_s, grad_z = grad_state
    _, numerator, denominator, scores_low, same_mask, carry_on, tail_mask, keep_gate = block_terms(
        (prior_s, previous_normalizer, prior_last), query_blk, key_blk, value_blk, seg_blk
    )
    result = numerator / denominator[..., None]
    grad_num = attn_blk / denominator[..., None]
    grad_den = -jnp.sum(attn_blk * result, axis=-1) / denominator
    grad_scores = jnp.einsum(
        "mthe,mshe->mhts", grad_num, value_blk, preferred_element_type=jnp.float32
    )
    grad_scores = (grad_scores + jnp.transpose(grad_den, (0, 2, 1))[..., None]) * same_mask[:, None]
    query_grad = jnp.einsum(
        "mhts,mshd->mthd", grad_scores, key_blk, preferred_element_type=jnp.float32
    )
    query_grad = query_grad + carry_on[:, :, None, None] * (
        jnp.einsum("mthe,mhde->mthd", grad_num, prior_s, precision=FULL_PRECISION)
        + grad_den[..., None] * previous_normalizer[:, None]
    )
    key_grad = jnp.einsum(
        "mhts,mthd->mshd", grad_scores, query_blk, preferred_element_type=jnp.float32
    )
    key_grad = key_grad + tail_mask[:, :, None, None] * (
        jnp.einsum(
            "mshe,mhde->mshd", value_blk.astype(jnp.float32), grad_s, precision=FULL_PRECISION
        )
        + grad_z[:, None]
    )
    value_grad = jnp.einsum(
        "mhts,mthe->mshe", scores_low, grad_num, preferred_element_type=jnp.float32
    )
    value_grad = value_grad + tail_mask[:, :, None, None] * jnp.einsum(
        "mshd,mhde->mshe", key_blk.astype(jnp.float32), grad_s, precision=FULL_PRECISION
    )
    query_on = query_blk.astype(jnp.float32) * carry_on[:, :, None, None]
    grad_s_in = keep_gate[:, None, None, None] * grad_s + jnp.einsum(
        "mthd,mthe->mhde", query_on, grad_num, precision=FULL_PRECISION
    )
    grad_z_in = keep_gate[:, None, None] * grad_z + jnp.sum(query_on * grad_den[..., None], axis=1)
    return ((grad_s_in, grad_z_in), (query_grad, key_grad, value_grad))


def join_states(earlier, later_part):
    keep_gate = (earlier[2] >= later_part[2]).astype(jnp.float32)
    return (
        later_part[0] + keep_gate[:, None, None, None] * earlier[0],
        later_part[1] + keep_gate[:, None, None] * earlier[1],
        jnp.maximum(earlier[2], later_part[2]),
    )


def compose_back(earlier, later_part):
    return (
        later_part[0] + later_part[2][:, None, None, None] * earlier[0],
        later_part[1] + later_part[2][:, None, None] * earlier[1],
        later_part[2] * earlier[2],
    )


def body(
    tokens,
    norm_gain,
    query_weight,
    key_weight,
    value_weight,
    attention_output_weight,
    feedforward_norm_gain,
    up_weight,
    down_weight,
    segment_ids,
    out_grad,
):
    batch, length, col_share = tokens.shape
    heads_here = query_weight.shape[1] // DH
    blocks_here = length // BLOCK
    head_index = lax.axis_index("head")

    def to_blocks(values):
        return jnp.moveaxis(values.reshape((batch, blocks_here, BLOCK) + values.shape[2:]), 1, 0)

    def from_blocks(values):
        return jnp.moveaxis(values, 0, 1).reshape((batch, length) + values.shape[3:])

    whole_in = lax.all_gather(tokens, "head", axis=2, tiled=True)
    unit_one, inv_one = normalize(whole_in.astype(jnp.float32))
    normed = (unit_one * norm_gain).astype(jnp.bfloat16)
    query_pre = jnp.einsum("mtd,dc->mtc", normed, query_weight, preferred_element_type=jnp.float32)
    key_pre = jnp.einsum("mtd,dc->mtc", normed, key_weight, preferred_element_type=jnp.float32)
    value_low = jnp.einsum(
        "mtd,dc->mtc", normed, value_weight, preferred_element_type=jnp.float32
    ).astype(jnp.bfloat16)
    query_feat = feature(query_pre).astype(jnp.bfloat16).reshape(batch, length, heads_here, DH)
    key_feat = feature(key_pre).astype(jnp.bfloat16).reshape(batch, length, heads_here, DH)
    value_per_head = value_low.reshape(batch, length, heads_here, DH)
    seg_float = segment_ids.astype(jnp.float32)
    own_last = seg_float[:, -1]
    tail_rows = (seg_float == own_last[:, None]).astype(jnp.float32)
    tail_keys = key_feat * tail_rows[:, :, None, None].astype(jnp.bfloat16)
    local_s = jnp.einsum(
        "mshd,mshe->mhde", tail_keys, value_per_head, preferred_element_type=jnp.float32
    )
    local_z = jnp.sum(tail_keys.astype(jnp.float32), axis=1)
    identity = (jnp.zeros_like(local_s), jnp.zeros_like(local_z), jnp.full_like(own_last, -1.0))
    prefix_s, prefix_z, prefix_last = prefix(
        (local_s, local_z, own_last), "seq", join_states, identity
    )
    block_inputs = (
        to_blocks(query_feat),
        to_blocks(key_feat),
        to_blocks(value_per_head),
        to_blocks(seg_float),
    )

    def forward_step(state_in, items):
        terms = block_terms(state_in, items[0], items[1], items[2], items[3])
        attn_blk = (terms[1] / terms[2][..., None]).astype(jnp.bfloat16)
        return (terms[0], (attn_blk, state_in[0], state_in[1], state_in[2]))

    _, (attn_blocks, saved_s, saved_z, saved_last) = lax.scan(
        forward_step, (prefix_s, prefix_z, prefix_last), block_inputs
    )
    attn_low = from_blocks(attn_blocks).reshape(batch, length, heads_here * DH)
    branch_part = jnp.einsum(
        "mtc,cd->mtd", attn_low, attention_output_weight, preferred_element_type=jnp.float32
    )
    branch = lax.psum_scatter(branch_part, "head", scatter_dimension=2, tiled=True)
    middle = tokens.astype(jnp.float32) + branch
    middle_full = lax.all_gather(middle.astype(jnp.bfloat16), "head", axis=2, tiled=True)
    unit_two, inv_two = normalize(middle_full.astype(jnp.float32))
    normed_two = (unit_two * feedforward_norm_gain).astype(jnp.bfloat16)
    hidden_pre = jnp.einsum(
        "mtd,df->mtf", normed_two, up_weight, preferred_element_type=jnp.float32
    )
    hidden = jax.nn.silu(hidden_pre).astype(jnp.bfloat16)
    ffn_part = jnp.einsum("mtf,fd->mtd", hidden, down_weight, preferred_element_type=jnp.float32)
    ffn_share = lax.psum_scatter(
        ffn_part.astype(jnp.bfloat16), "head", scatter_dimension=2, tiled=True
    ).astype(jnp.float32)
    layer_out = (middle + ffn_share).astype(jnp.bfloat16)
    grad_full = lax.all_gather(out_grad, "head", axis=2, tiled=True)
    down_weight_grad = jnp.einsum(
        "mtf,mtd->fd", hidden, grad_full, preferred_element_type=jnp.float32
    )
    hidden_act = jnp.einsum(
        "mtd,fd->mtf", grad_full, down_weight, preferred_element_type=jnp.float32
    )
    hidden_grad = (hidden_act * silu_slope(hidden_pre)).astype(jnp.bfloat16)
    up_weight_grad = jnp.einsum(
        "mtd,mtf->df", normed_two, hidden_grad, preferred_element_type=jnp.float32
    )
    norm_two_part = jnp.einsum(
        "mtf,df->mtd", hidden_grad, up_weight, preferred_element_type=jnp.float32
    )
    middle_norm, ffn_gain_grad = norm_back(
        norm_two_part, unit_two, inv_two, feedforward_norm_gain, col_share, head_index
    )
    middle_grad = out_grad.astype(jnp.float32) + middle_norm
    middle_full_grad = lax.all_gather(middle_grad.astype(jnp.bfloat16), "head", axis=2, tiled=True)
    out_weight_grad = jnp.einsum(
        "mtc,mtd->cd", attn_low, middle_full_grad, preferred_element_type=jnp.float32
    )
    attn_grad = jnp.einsum(
        "mtd,cd->mtc", middle_full_grad, attention_output_weight, preferred_element_type=jnp.float32
    )
    attn_grad_blocks = to_blocks(attn_grad.reshape(batch, length, heads_here, DH))
    zero_state = (jnp.zeros_like(local_s), jnp.zeros_like(local_z))
    (own_gs, own_gz), (qgrad_blocks, kgrad_blocks, vgrad_blocks) = lax.scan(
        block_back,
        zero_state,
        block_inputs + (saved_s, saved_z, saved_last, attn_grad_blocks),
        reverse=True,
    )
    pass_gate = (prefix_last >= own_last).astype(jnp.float32)
    identity_back = (jnp.zeros_like(own_gs), jnp.zeros_like(own_gz), jnp.ones_like(own_last))
    later_s, later_z, _ = carried_in(
        (own_gs, own_gz, pass_gate), "seq", compose_back, identity_back
    )
    key_wide = key_feat.astype(jnp.float32)
    value_wide = value_per_head.astype(jnp.float32)
    tail_wide = tail_rows[:, :, None, None]
    kfeat_grad = from_blocks(kgrad_blocks) + tail_wide * (
        jnp.einsum("mshe,mhde->mshd", value_wide, later_s, precision=FULL_PRECISION)
        + later_z[:, None]
    )
    value_act = from_blocks(vgrad_blocks) + tail_wide * jnp.einsum(
        "mshd,mhde->mshe", key_wide, later_s, precision=FULL_PRECISION
    )
    qfeat_grad = from_blocks(qgrad_blocks)
    query_low_grad = (
        qfeat_grad.reshape(batch, length, heads_here * DH) * feature_slope(query_pre)
    ).astype(jnp.bfloat16)
    key_low_grad = (
        kfeat_grad.reshape(batch, length, heads_here * DH) * feature_slope(key_pre)
    ).astype(jnp.bfloat16)
    value_low_grad = value_act.reshape(batch, length, heads_here * DH).astype(jnp.bfloat16)
    query_weight_grad = jnp.einsum(
        "mtd,mtc->dc", normed, query_low_grad, preferred_element_type=jnp.float32
    )
    key_weight_grad = jnp.einsum(
        "mtd,mtc->dc", normed, key_low_grad, preferred_element_type=jnp.float32
    )
    value_weight_grad = jnp.einsum(
        "mtd,mtc->dc", normed, value_low_grad, preferred_element_type=jnp.float32
    )
    norm_one_part = jnp.einsum(
        "mtc,dc->mtd", query_low_grad, query_weight, preferred_element_type=jnp.float32
    )
    norm_one_part = norm_one_part + jnp.einsum(
        "mtc,dc->mtd", key_low_grad, key_weight, preferred_element_type=jnp.float32
    )
    norm_one_part = norm_one_part + jnp.einsum(
        "mtc,dc->mtd", value_low_grad, value_weight, preferred_element_type=jnp.float32
    )
    input_norm, norm_gain_grad = norm_back(
        norm_one_part, unit_one, inv_one, norm_gain, col_share, head_index
    )
    input_grad = middle_grad + input_norm
    totals = lax.psum(
        (
            query_weight_grad,
            key_weight_grad,
            value_weight_grad,
            out_weight_grad,
            up_weight_grad,
            down_weight_grad,
            norm_gain_grad,
            ffn_gain_grad,
        ),
        "seq",
    )
    return (
        layer_out,
        input_grad,
        totals[6],
        totals[0],
        totals[1],
        totals[2],
        totals[3],
        totals[7],
        totals[4],
        totals[5],
    )


def solution(mesh):
    in_specs = (
        P(None, "seq", "head"),
        P(),
        P(None, "head"),
        P(None, "head"),
        P(None, "head"),
        P("head", None),
        P(),
        P(None, "head"),
        P("head", None),
        P(None, "seq"),
        P(None, "seq", "head"),
    )
    out_specs = (
        P(None, "seq", "head"),
        P(None, "seq", "head"),
        P("head"),
        P(None, "head"),
        P(None, "head"),
        P(None, "head"),
        P("head", None),
        P("head"),
        P(None, "head"),
        P("head", None),
    )
    return jax.shard_map(body, mesh=mesh, in_specs=in_specs, out_specs=out_specs, check_vma=False)
```

profile of v0, /device:TPU:0, one launch (start us, length us, event | category | flops | bytes accessed | tf_op | source)
XLA Modules:
  0.0 652.7 jit_solution(14915657804589845892)
XLA Ops:
  9.7 25.5 %all-gather.11.cloned.1.call-done = bf16[8,256,512]{2,1,0:T(8,128)(2,1)} async-done(((bf16[8,256,128]{2,1,0:T(8,128)(2,1)}), bf16[8,256,512]{2,1,0:T(8,128)(2,1)}) %all-gather.11.cloned.1.call-update) | async-done | bytes 2097168 | tf_op jit(solution)/shard_map/all_gather | solution.py:223
  47.6 21.6 %all-reduce = f32[64]{0:T(128)S(1)} all-reduce(f32[64]{0:T(128)S(1)} %dynamic-update-slice), channel_id=3, replica_groups=mesh['seq'=8,'head'=4] {'seq'}, use_global_device_ids=true, to_apply=%add | all-reduce | flops 64 | bytes 512
  69.7 31.0 %all_gather.48 = f32[8,8,2,64]{3,1,2,0:T(8,128)S(1)} all-gather(f32[1,8,2,64]{3,1,2,0:T(8,128)S(1)} %copy.73), channel_id=1, replica_groups=mesh['seq'=8,'head'=4] {'seq'}, dimensions={0}, use_global_device_ids=true | all-gather | bytes 36864 | tf_op jit(solution)/shard_map/all_gather | solution.py:16
  109.7 10.5 %all-gather.19.cloned.1.call-done = f32[64,2,64,64]{3,2,1,0:T(8,128)} async-done(((f32[8,2,64,64]{3,2,1,0:T(8,128)}), f32[64,2,64,64]{3,2,1,0:T(8,128)}) %all-gather.19.cloned.1.call-update) | async-done | bytes 2097168 | tf_op jit(solution)/shard_map/all_gather | solution.py:16
  120.2 15.8 %while.23 = (s32[]{:T(128)}, f32[8,2,64,64]{3,2,1,0:T(8,128)}, f32[8,2,64]{2,1,0:T(2,128)S(1)}, f32[8]{0:T(128)S(1)}, s32[]{:T(128)}, /*index=5*/f32[8,8,2,64,64...) while((s32[]{:T(128)}, f32[8,2,64,64]{3,2,1,0:T(8,128)}, ...), condition=%wide.region_4.5_spmd.clone, body=%wide.region_3.4_spmd.clone.sunk | while | flops 266292 | bytes 807310 | solution.py:25
  144.3 43.1 %reduce-scatter.7.cloned.1.call-done = f32[8,256,128]{2,1,0:T(8,128)} async-done(((f32[8,256,512]{2,1,0:T(8,128)}), f32[8,256,128]{2,1,0:T(8,128)}) %reduce-scatter.7.cloned.1.call-update) | async-done | bytes 1048592 | tf_op jit(solution)/shard_map/reduce_scatter | solution.py:265
  190.5 22.2 %all-gather.13.cloned.1.call-done = bf16[8,256,512]{2,1,0:T(8,128)(2,1)} async-done(((bf16[8,256,128]{2,1,0:T(8,128)(2,1)}), bf16[8,256,512]{2,1,0:T(8,128)(2,1)}) %all-gather.13.cloned.1.call-update) | async-done | bytes 2097168 | tf_op jit(solution)/shard_map/all_gather | solution.py:267
  217.3 3.9 multiply_convert_fusion.1
  221.1 15.9 %all-gather.15.cloned.1.call-done = bf16[8,256,512]{2,1,0:T(8,128)(2,1)} async-done(((bf16[8,256,128]{2,1,0:T(8,128)(2,1)}), bf16[8,256,512]{2,1,0:T(8,128)(2,1)}) %all-gather.15.cloned.1.call-update) | async-done | bytes 2097168 | tf_op jit(solution)/shard_map/all_gather | solution.py:279
  237.0 5.2 multiply_convert_fusion
  250.7 40.9 %reduce-scatter.9.cloned.1.call-done = f32[8,256,128]{2,1,0:T(8,128)} async-done(((f32[8,256,512]{2,1,0:T(8,128)}), f32[8,256,128]{2,1,0:T(8,128)}) %reduce-scatter.9.cloned.1.call-update) | async-done | bytes 1048592 | tf_op jit(solution)/shard_map/reduce_scatter | solution.py:75
  294.4 10.9 %all-reduce.5 = (f32[8,256]{1,0:T(8,128)S(1)}, f32[8,256]{1,0:T(8,128)}) all-reduce(f32[8,256]{1,0:T(8,128)S(1)} %get-tuple-element.493, f32[8,256]{1,0:T(8,128)S(1)} %get-tuple-element.497), channel_id=1, replica_groups=mesh['seq'=8,'head'=4] {'head'}, use_global_device_ids=true, to_apply=%region_14.15 | all-reduce | flops 4096 | bytes 32768 | tf_op jit(solution)/shard_map/psum | solution.py:78
  309.0 24.0 %all-gather.17.cloned.1.call-done = bf16[8,256,512]{2,1,0:T(8,128)(2,1)} async-done(((bf16[8,256,128]{2,1,0:T(8,128)(2,1)}), bf16[8,256,512]{2,1,0:T(8,128)(2,1)}) %all-gather.17.cloned.1.call-update) | async-done | bytes 2097168 | tf_op jit(solution)/shard_map/all_gather | solution.py:297
  342.2 21.7 %all-reduce.1 = bf16[64]{0:T(256)(128)(2,1)S(1)} all-reduce(bf16[64]{0:T(256)(128)(2,1)S(1)} %dynamic-update-slice.1), channel_id=5, replica_groups=mesh['seq'=8,'head'=4] {'seq'}, use_global_device_ids=true, to_apply=%add.1 | all-reduce | flops 64 | bytes 256
  364.6 4.3 convolution_convert_fusion
  368.9 4.6 copy.124
  387.7 31.3 %all_gather.56 = bf16[8,8,2,64]{3,1,2,0:T(8,128)(2,1)} all-gather(bf16[1,8,2,64]{3,1,2,0:T(8,128)(2,1)S(1)} %copy.82), channel_id=1, replica_groups=mesh['seq'=8,'head'=4] {'seq'}, dimensions={0}, use_global_device_ids=true | all-gather | bytes 18432 | tf_op jit(solution)/shard_map/all_gather | solution.py:31
  426.0 20.6 %while.24 = (s32[]{:T(128)}, f32[8,2,64,64]{3,2,1,0:T(8,128)S(1)}, f32[8,2,64]{2,1,0:T(2,128)S(1)}, s32[]{:T(128)}, bf16[8,8,2,64,64]{4,3,2,1,0:T(8,128)(2,1)}, ...) while((s32[]{:T(128)}, f32[8,2,64,64]{3,2,1,0:T(8,128)S(1)}, ...), condition=%wide.region_18.19_spmd.clone, body=%wide.region_17.18_spmd.clone.sunk | while | flops 332816 | bytes 669997 | solution.py:49
  459.2 4.1 convolution_bitcast_fusion
  480.2 18.5 %reduce-scatter.11.cloned.1.call-done = f32[8,256,128]{2,1,0:T(8,128)} async-done(((f32[8,256,512]{2,1,0:T(8,128)}), f32[8,256,128]{2,1,0:T(8,128)}) %reduce-scatter.11.cloned.1.call-update) | async-done | bytes 1048592 | tf_op jit(solution)/shard_map/reduce_scatter | solution.py:75
  500.9 22.3 %all-reduce.2 = (f32[128]{0:T(128)}, f32[128]{0:T(128)}) all-reduce(f32[128]{0:T(128)S(1)} %get-tuple-element.494, f32[128]{0:T(128)S(1)} %copy-done.56), channel_id=1, replica_groups=mesh['seq'=8,'head'=4] {'seq'}, use_global_device_ids=true, to_apply=%region_25.26 | all-reduce | flops 256 | bytes 2048 | tf_op jit(solution)/shard_map/psum | solution.py:357
  523.2 10.9 %all-reduce.4 = (f32[8,256]{1,0:T(8,128)S(1)}, f32[8,256]{1,0:T(8,128)S(1)}) all-reduce(f32[8,256]{1,0:T(8,128)S(1)} %get-tuple-element.495, f32[8,256]{1,0:T(8,128)S(1)} %get-tuple-element.496), channel_id=1, replica_groups=mesh['seq'=8,'head'=4] {'head'}, use_global_device_ids=true, to_apply=%region_23.24 | all-reduce | flops 4096 | bytes 32768 | tf_op jit(solution)/shard_map/psum | solution.py:78
  534.2 4.8 multiply_add_fusion
  539.0 96.8 %all-reduce.8.cloned.1.call-done = (f32[512,128]{1,0:T(8,128)}, f32[512,128]{1,0:T(8,128)}, f32[512,128]{1,0:T(8,128)}, f32[128,512]{1,0:T(8,128)}, f32[512,512]{1,0:T(8,128)}, /*index=5*/f32[512,512]{1,0:T(8,128)}) async-done(((f32[512,128]{1,0:T(8,128)}, f32[512,128]{1,0:T(8,128)}, f32[512,128]{1,0:T(8,128)}, f32[128,512]{1,0:T(8,128)}, f32[512,512]{1,0:T(8,128)}, /*index=5*/f32[512,512]{1,0:T(8,128)}), ...) | async-done | bytes 3145744 | tf_op jit(solution)/shard_map/psum | solution.py:357
  (305 shorter events, 162.6 us)
Async XLA Ops:
  7.2 210.1 %copy-start = (bf16[512,512]{1,0:T(8,128)(2,1)S(1)}, bf16[512,512]{1,0:T(8,128)(2,1)}, u32[]{:S(2)}) copy-start(bf16[512,512]{1,0:T(8,128)(2,1)} %param.22) | copy-start | bytes 1572868
  7.2 32.6 %copy-start.60 = (f32[512]{0:T(512)S(1)}, f32[512]{0:T(512)}, u32[]{:S(2)}) copy-start(f32[512]{0:T(512)} %param.16) | copy-start | bytes 6148
  7.2 32.6 %copy-start.41 = (bf16[512,128]{1,0:T(8,128)(2,1)S(1)}, bf16[512,128]{1,0:T(8,128)(2,1)}, u32[]{:S(2)}) copy-start(bf16[512,128]{1,0:T(8,128)(2,1)} %param.18) | copy-start | bytes 393220
  7.2 28.0 %all-gather.11.cloned.1.call-start = ((), (), s32[]{:S(2)}) async-start(), calls=%async_computation.4 | async-start | bytes 2621440 | tf_op jit(solution)/shard_map/all_gather | solution.py:223
  8.0 112.2 %all-gather.19.cloned.1.call-start = ((), (), s32[]{:S(2)}) async-start(), calls=%async_computation.11 | async-start | bytes 4718592 | tf_op jit(solution)/shard_map/all_gather | solution.py:16
  8.9 38.4 %copy-start.54 = (f32[8]{0:T(128)}, f32[8]{0:T(128)S(1)}, u32[]{:S(2)}) copy-start(f32[8]{0:T(128)S(1)} %slice_reduce_fusion) | copy-start | bytes 100
  46.0 141.5 %reduce-scatter.7.cloned.1.call-start = ((), (), s32[]{:S(2)}) async-start(), calls=%async_computation.5 | async-start | bytes 5242880 | tf_op jit(solution)/shard_map/reduce_scatter | solution.py:265
  144.3 73.0 %copy-start.58 = (f32[512]{0:T(512)S(1)}, f32[512]{0:T(512)}, u32[]{:S(2)}) copy-start(f32[512]{0:T(512)} %param.21) | copy-start | bytes 6148
  144.3 68.4 %all-gather.13.cloned.1.call-start = ((), (), s32[]{:S(2)}) async-start(), calls=%async_computation.6 | async-start | bytes 2621440 | tf_op jit(solution)/shard_map/all_gather | solution.py:267
  189.7 47.3 %all-gather.15.cloned.1.call-start = ((), (), s32[]{:S(2)}) async-start(), calls=%async_computation.7 | async-start | bytes 2621440 | tf_op jit(solution)/shard_map/all_gather | solution.py:279
  190.3 101.4 %reduce-scatter.9.cloned.1.call-start = ((), (), s32[]{:S(2)}) async-start(), calls=%async_computation.8 | async-start | bytes 5242880 | tf_op jit(solution)/shard_map/reduce_scatter | solution.py:75
  214.8 32.4 %copy-start.43 = (f32[8,256]{1,0:T(8,128)}, f32[8,256]{1,0:T(8,128)S(1)}, u32[]{:S(2)}) copy-start(f32[8,256]{1,0:T(8,128)S(1)} %broadcast_multiply_fusion.2) | copy-start | bytes 24580
  247.0 85.9 %all-gather.17.cloned.1.call-start = ((), (), s32[]{:S(2)}) async-start(), calls=%async_computation.9 | async-start | bytes 2621440 | tf_op jit(solution)/shard_map/all_gather | solution.py:297
  247.2 44.5 %copy-start.52 = (f32[128]{0:T(128)}, f32[128]{0:T(128)S(1)}, u32[]{:S(2)}) copy-start(f32[128]{0:T(128)S(1)} %dynamic_slice.93) | copy-start | bytes 1540
  294.4 42.2 %copy-start.20 = (bf16[8,256,128]{1,2,0:T(8,128)(2,1)S(1)}, bf16[8,256,128]{1,2,0:T(8,128)(2,1)}, u32[]{:S(2)}) copy-start(bf16[8,256,128]{1,2,0:T(8,128)(2,1)} %copy-done.19) | copy-start | bytes 1572868
  309.0 117.0 %all-gather.21.cloned.1.call-start = ((), (), s32[]{:S(2)}) async-start(), calls=%async_computation.12 | async-start | bytes 2359296 | tf_op jit(solution)/shard_map/all_gather | solution.py:31
  339.3 137.0 %reduce-scatter.13.cloned.1.call-start = ((), (), s32[]{:S(2)}) async-start(), calls=%async_computation.13 | async-start | bytes 2621440
  377.1 121.6 %reduce-scatter.11.cloned.1.call-start = ((), (), s32[]{:S(2)}) async-start(), calls=%async_computation.10 | async-start | bytes 5242880 | tf_op jit(solution)/shard_map/reduce_scatter | solution.py:75
  457.7 178.1 %all-reduce.8.cloned.1.call-start = ((), (), s32[]{:S(2)}) async-start(), calls=%async_computation.14 | async-start | bytes 6291456 | tf_op jit(solution)/shard_map/psum | solution.py:357
  476.3 57.9 %copy-start.13 = (f32[8,256,128]{2,1,0:T(8,128)S(1)}, f32[8,256,128]{2,1,0:T(8,128)}, u32[]{:S(2)}) copy-start(f32[8,256,128]{2,1,0:T(8,128)} %reduce-scatter.9.cloned.1.call-done) | copy-start | bytes 3145732
  476.3 57.9 %copy-start.24 = (bf16[8,256,128]{2,1,0:T(8,128)(2,1)S(1)}, bf16[8,256,128]{2,1,0:T(8,128)(2,1)}, u32[]{:S(2)}) copy-start(bf16[8,256,128]{2,1,0:T(8,128)(2,1)} %param.25) | copy-start | bytes 1572868
  476.3 57.9 %copy-start.51 = (f32[8,256]{1,0:T(8,128)S(1)}, f32[8,256]{1,0:T(8,128)}, u32[]{:S(2)}) copy-start(f32[8,256]{1,0:T(8,128)} %copy-done.50) | copy-start | bytes 24580
  476.3 57.9 %copy-start.53 = (f32[128]{0:T(128)S(1)}, f32[128]{0:T(128)}, u32[]{:S(2)}) copy-start(f32[128]{0:T(128)} %copy-done.52) | copy-start | bytes 1540
  534.2 111.6 %copy-start.1 = (bf16[512,512]{1,0:T(8,128)(2,1)S(1)}, bf16[512,512]{1,0:T(8,128)(2,1)}, u32[]{:S(2)}) copy-start(bf16[512,512]{1,0:T(8,128)(2,1)} %param.22) | copy-start | bytes 1572868
  (50 other events, 229.8 us)
Sparse Core Ops, SparseCore 0:
  9.6 25.5 all-gather.10
  46.1 74.0 all-gather.18
  144.4 43.0 reduce-scatter.6
  189.8 22.8 all-gather.12
  214.2 22.8 all-gather.14
  247.2 44.4 reduce-scatter.8
  309.1 23.8 all-gather.16
  339.4 49.4 all-gather.20
  391.4 29.9 reduce-scatter.12
  457.8 40.8 reduce-scatter.10
  504.1 131.5 all-reduce.7
where the time goes:
time: 661 us; the launch traced here: 653 us
  waiting for transfers between devices  299 us (45%)
  blocking collectives  150 us (23%)
  matrix products  80.6 us (12%)
  other arithmetic  66.9 us (10%)
  local copies, waits for them, and re-layouts  39.8 us (6%)
  between operations  15.8 us (2%)
    psum x1, waiting for transfers between devices, body(): lax.psum((query_weight_grad, key_weight_grad, value_weight_grad, out_weig...  96.8 us
    reduce_scatter x2, waiting for transfers between devices, norm_back(): lax.psum_scatter(grad_part, 'head', scatter_dimension=2, tiled=True)  59.4 us
    unnamed x2, blocking collectives  43.4 us
    reduce_scatter x1, waiting for transfers between devices, body(): lax.psum_scatter(branch_part, 'head', scatter_dimension=2, tiled=True)  43.1 us
    unnamed x141, local copies, waits for them, and re-layouts  33 us
    all_gather x1, blocking collectives, carried_in(): lax.all_gather(part.astype(kind), axis)  31.3 us
    all_gather x1, blocking collectives, prefix(): pieces = jax.tree.map(lambda part: lax.all_gather(part, axis), value)  31 us
    all_gather x1, waiting for transfers between devices, body(): whole_in = lax.all_gather(tokens, 'head', axis=2, tiled=True)  25.5 us
  transfers between devices with their start and end apart: 11, of which 9 were waited for; matrix products, arithmetic and copies ran while one was open for 17% of the time, Pallas kernels for 0%

commit v1 on v0

v1 whole, which is shorter than its diff:
```python
import functools

import jax
import jax.numpy as jnp
from jax import lax
from jax.experimental import pallas as pl
from jax.experimental.pallas import tpu as pltpu
from jax.sharding import PartitionSpec as P

DH = 64
BLOCK = 256
EPSILON = 1e-05
MESH = pl.DeviceIdType.MESH
F32 = jnp.float32
BF16 = jnp.bfloat16
MIB = 1 << 20

KINDS = 4
UNITS = 3


def mm(left, right, form="NN"):
    dims = {"NN": ((1,), (0,)), "NT": ((1,), (1,)), "TN": ((0,), (0,))}[form]
    return lax.dot_general(left, right, (dims, ((), ())), preferred_element_type=F32)


def loop(count, step):
    def run(i, carry):
        step(i)
        return carry

    lax.fori_loop(0, count, run, 0)


def rows_loop(total, chunk, step):
    loop(total // chunk, lambda i: step(pl.ds(pl.multiple_of(i * chunk, chunk), chunk)))


def at128(i):
    return pl.ds(pl.multiple_of(i * 128, 128), 128)


def layer_kernel(
    pairs,
    tok,
    og_in,
    wq,
    wk,
    wv,
    wo,
    wu,
    wd,
    seg,
    gain_one,
    gain_two,
    lo_out,
    ig_out,
    fin,
    gains,
    xin,
    ogs,
    w_qkv,
    w_o,
    w_u,
    w_d,
    seg_other,
    unit_one,
    unit_two,
    rstd_one,
    rstd_two,
    normed,
    normed_two,
    feat,
    val,
    mask,
    mask_t,
    seg_col,
    carry_on,
    own_s,
    own_z,
    msg_s,
    msg_z,
    buf_s,
    buf_z,
    state,
    attn,
    attn_wide,
    den_inv,
    middle,
    work,
    work_two,
    hid,
    hid_grad,
    ffn,
    norm_grad,
    middle_grad,
    middle_low,
    num_grad,
    den_grad,
    grad_s,
    grad_z,
    msg_gs,
    msg_gz,
    buf_gs,
    buf_gz,
    key_acc,
    val_acc,
    low_grads,
    lo_s,
    ig_s,
    part,
    buf_core,
    buf_y,
    buf_x,
    buf_ring,
    own_piece,
    gain_part,
    gain_buf,
    local_sem,
    send_sem,
    recv_sem,
):
    s = lax.axis_index("seq")
    h = lax.axis_index("head")
    pair, par = lax.div(s, 2), lax.rem(s, 2)
    hy, hc = lax.div(h, 2), lax.rem(h, 2)
    member = par * 4 + h
    others = pairs - 1

    ids = iter(range(10000))
    sends = []

    def peer(dp, dy, dc):
        par_to = 1 - par if dp else par
        y_to = 1 - hy if dy else hy
        c_to = 1 - hc if dc else hc
        return par_to, y_to, c_to

    def address(par_to, y_to, c_to):
        return (2 * pair + par_to, 2 * y_to + c_to)

    core, ypeer, xpeer = (address(*peer(*d)) for d in ((0, 0, 1), (0, 1, 0), (1, 0, 0)))

    def ring(d):
        to = lax.rem(pair + d, pairs)
        return to, (2 * to + par, h)

    def remote(src, dst, device):
        i = next(ids)
        return pltpu.make_async_remote_copy(
            src_ref=src,
            dst_ref=dst,
            send_sem=send_sem.at[i],
            recv_sem=recv_sem.at[i],
            device_id=device,
            device_id_type=MESH,
        )

    def start(copy):
        copy.start()
        sends.append(copy)
        return copy

    local_ids = iter(range(1000))

    def local(src, dst):
        copy = pltpu.make_async_copy(src, dst, local_sem.at[next(local_ids)])
        copy.start()
        return copy

    hcol = at128(h)
    own_tok = local(tok.at[member], xin.at[pl.ds(pl.multiple_of(par * 256, 256), 256), hcol])
    own_w = [
        [local(w, w_qkv.at[i, :, hcol]) for i, w in enumerate((wq, wk, wv))],
        [local(wo, w_o.at[hcol])],
        [local(wu, w_u.at[h])],
        [local(wd, w_d.at[h])],
    ]
    own_og = local(og_in.at[member], ogs.at[pl.ds(pl.multiple_of(par * 256, 256), 256), hcol])
    row8 = lax.broadcasted_iota(jnp.int32, (8, 128), 0)
    neutral = jnp.where(row8 == 4, -1.0, 0.0).astype(F32)
    for slot in range(2):
        buf_s[slot] = jnp.zeros((256, 128), BF16)
        buf_gs[slot] = jnp.zeros((256, 128), BF16)
        buf_z[slot] = neutral
        buf_gz[slot] = jnp.zeros((8, 128), F32)

    barrier = pltpu.get_barrier_semaphore()
    combos = [(1, 0, 0), (0, 1, 0), (1, 1, 0), (1, 0, 1), (0, 1, 1), (1, 1, 1), (0, 0, 1)]
    for d in combos:
        pl.semaphore_signal(
            barrier, inc=1, device_id=address(*peer(*d)), device_id_type=MESH
        )
    for d in range(1, pairs):
        pl.semaphore_signal(barrier, inc=1, device_id=ring(d)[1], device_id_type=MESH)
    pl.semaphore_wait(barrier, 7 + others)

    def scatter_in(src, dst):
        copies = []
        for d in combos:
            par_to, y_to, c_to = peer(*d)
            copies.append(
                start(
                    remote(
                        src.at[par_to * 4 + 2 * y_to + c_to],
                        dst.at[pl.ds(pl.multiple_of(par * 256, 256), 256), hcol],
                        address(par_to, y_to, c_to),
                    )
                )
            )
        return copies

    def scatter_out(src, dst):
        copies = []
        for d in combos:
            par_to, y_to, c_to = peer(*d)
            copies.append(
                start(
                    remote(
                        src.at[
                            pl.ds(pl.multiple_of(par_to * 256, 256), 256),
                            at128(2 * y_to + c_to),
                        ],
                        dst.at[member],
                        address(par_to, y_to, c_to),
                    )
                )
            )
        own = local(src.at[pl.ds(pl.multiple_of(par * 256, 256), 256), hcol], dst.at[member])
        return copies, own

    half256 = pl.ds(pl.multiple_of(par * 256, 256), 256)

    def view(kind, shard, half):
        if kind == 0:
            rows = (
                slice(None)
                if half is None
                else pl.ds(pl.multiple_of(half * 256, 256), 256)
            )
            return w_qkv.at[:, rows, at128(shard)]
        if kind == 1:
            if half is None:
                return w_o.at[at128(shard)]
            return w_o.at[pl.ds(pl.multiple_of(shard * 128 + half * 64, 64), 64)]
        ref = w_u if kind == 2 else w_d
        if half is None:
            return ref.at[shard]
        return ref.at[shard, pl.ds(pl.multiple_of(half * 256, 256), 256)]

    across = 2 * (1 - hy) + hc

    def weight_y(kind):
        return start(remote(view(kind, h, par), view(kind, h, par), ypeer))

    def weight_core(kind):
        return start(remote(view(kind, h, None), view(kind, h, None), core))

    def weight_x(kind):
        x = start(remote(view(kind, across, par), view(kind, across, par), xpeer))
        c = start(remote(view(kind, across, par), view(kind, across, par), core))
        return x, c

    def weight_last(kind):
        return start(remote(view(kind, across, 1 - par), view(kind, across, 1 - par), core))

    for copy in own_w[0]:
        copy.wait()
    wy = {0: weight_y(0)}
    wc = {0: weight_core(0)}
    tokens_in = scatter_in(tok, xin)
    seg_copy = start(remote(seg, seg_other, xpeer))
    for kind in (1, 2, 3):
        for copy in own_w[kind]:
            copy.wait()
        wc[kind] = weight_core(kind)
    wx, wl = {}, {}

    def forward_y(kind):
        wy[kind].wait_recv()
        wx[kind] = weight_x(kind)

    def forward_x(kind):
        wx[kind][0].wait_recv()
        wl[kind] = weight_last(kind)

    def weights_ready(kind):
        wc[kind].wait_recv()
        wx[kind][1].wait_recv()
        wl[kind].wait_recv()

    forward_y(0)
    for copy in tokens_in:
        copy.wait_recv()
    own_tok.wait()
    wy[1] = weight_y(1)
    wy[2] = weight_y(2)

    def norm_rows(source, gain, unit_ref, rstd_ref, out_ref):
        def step(r):
            x = source(r)
            center = x - jnp.mean(x, axis=-1, keepdims=True)
            scale = lax.rsqrt(jnp.mean(center * center, axis=-1, keepdims=True) + EPSILON)
            unit = center * scale
            unit_ref[r, :] = unit
            rstd_ref[r, :] = jnp.broadcast_to(scale, (unit.shape[0], 128))
            out_ref[r, :] = (unit * gain[...]).astype(BF16)

        rows_loop(512, 64, step)

    norm_rows(lambda r: xin[r, :].astype(F32), gain_one, unit_one, rstd_one, normed)

    seg_copy.wait_recv()
    own_row = seg[pl.ds(member, 1), :]
    other_row = seg_other[pl.ds(member, 1), :]
    seg_rows = (
        (own_row * (1 - par) + other_row * par).astype(F32),
        (own_row * par + other_row * (1 - par)).astype(F32),
    )
    first = lax.broadcasted_iota(jnp.int32, (256, 256), 0)
    second = lax.broadcasted_iota(jnp.int32, (256, 256), 1)
    for b in range(2):
        along = jnp.broadcast_to(seg_rows[b], (256, 256))
        down = along.T
        same = along == down
        mask[b] = jnp.where(same & (second <= first), 1.0, 0.0)
        mask_t[b] = jnp.where(same & (first <= second), 1.0, 0.0)
        seg_col[b] = down[:, :128]

    forward_x(0)
    weights_ready(0)

    def project(i):
        work[...] = mm(normed[...], w_qkv[i])

        def step(r):
            v = work[r, :]
            feat[i, r, :] = jnp.where(v > 0, v + 1.0, jnp.exp(jnp.minimum(v, 0.0))).astype(BF16)

        rows_loop(512, 64, step)

    val[...] = mm(normed[...], w_qkv[2]).astype(BF16)
    loop(2, lambda i: project(1 - i))

    lane = lax.broadcasted_iota(jnp.int32, (1, 128), 1)
    low_lanes = lane < 64
    spread = (
        lax.broadcasted_iota(jnp.int32, (128, 128), 0) // 64
        == lax.broadcasted_iota(jnp.int32, (128, 128), 1) // 64
    )

    def place(i):
        b, pr = lax.div(i, 4), lax.rem(i, 4)
        return b, pr, pl.ds(pl.multiple_of(b * 256, 256), 256), at128(pr)

    def pack(square):
        return jnp.where(low_lanes, square[:64], square[64:])

    def unpack(packed):
        zero = jnp.zeros_like(packed)
        return jnp.concatenate(
            [jnp.where(low_lanes, packed, zero), jnp.where(low_lanes, zero, packed)], axis=0
        )

    def two(rows):
        zero = jnp.zeros_like(rows)
        return jnp.concatenate(
            [jnp.where(low_lanes, rows, zero), jnp.where(low_lanes, zero, rows)], axis=0
        )

    def pick(stacked):
        return jnp.where(low_lanes, stacked[:256], stacked[256:])

    def packed_rows(pr):
        return pl.ds(pl.multiple_of(pr * 64, 64), 64)

    last_rows = [seg_col[b, pl.ds(255, 1), :] for b in range(2)]

    def own_state(i):
        b, pr, rows, cols = place(i)
        tail = seg_col[b] == seg_col[b, pl.ds(255, 1), :]
        keys = feat[1, rows, cols].astype(F32)
        keys = jnp.where(tail, keys, 0.0)
        own_s[b, packed_rows(pr), :] = pack(mm(keys.astype(BF16), val[rows, cols], "TN"))
        own_z[b, pl.ds(pr, 1), :] = jnp.sum(keys, axis=0, keepdims=True)

    own_z[...] = jnp.zeros_like(own_z)
    loop(8, own_state)
    keep_mid = jnp.where(last_rows[0] >= last_rows[1], 1.0, 0.0)
    msg_s[...] = (own_s[1] + keep_mid * own_s[0]).astype(BF16)
    msg_z[...] = jnp.where(row8 == 4, last_rows[1], own_z[1] + keep_mid * own_z[0])

    def shift(d, s_ref, z_ref, s_buf, z_buf, slot):
        to = lax.rem(pair + d + pairs, pairs)
        device = (2 * to + par, h)
        return (
            remote(s_ref, s_buf.at[slot], device),
            remote(z_ref, z_buf.at[slot], device),
        )

    forward = [shift(d, msg_s, msg_z, buf_s, buf_z, d - 1) for d in (1, 2)]
    for d, copies in zip((1, 2), forward):

        @pl.when(pair + d < pairs)
        def _():
            for copy in copies:
                copy.start()

    forward_y(1)
    forward_y(2)
    og_copies = scatter_in(og_in, ogs)
    wy[3] = weight_y(3)

    for d, copies in zip((1, 2), forward):

        @pl.when(pair >= d)
        def _():
            for copy in copies:
                copy.wait_recv()

    last_in = buf_z[0, pl.ds(4, 1), :]
    keep_in = jnp.where(buf_z[1, pl.ds(4, 1), :] >= last_in, 1.0, 0.0)
    keep_first = jnp.where(last_in >= last_rows[0], 1.0, 0.0)
    buf_z[0] = buf_z[0] + keep_in * buf_z[1]
    carry_on[0] = jnp.where(seg_col[0] == last_in, 1.0, 0.0)
    carry_on[1] = jnp.where(seg_col[1] == last_rows[0], 1.0, 0.0)

    def enter(pr):
        entering = buf_s[0, packed_rows(pr), :].astype(F32) + keep_in * buf_s[
            1, packed_rows(pr), :
        ].astype(F32)
        z_in = buf_z[0, pl.ds(pr, 1), :]
        middle_s = own_s[0, packed_rows(pr), :] + keep_first * entering
        middle_z = own_z[0, pl.ds(pr, 1), :] + keep_first * z_in
        for b, (packed, z_row) in enumerate(((entering, z_in), (middle_s, middle_z))):
            wide = jnp.where(spread, jnp.broadcast_to(z_row, (128, 128)).T, 0.0)
            state[b * 4 + pr, :, :128] = unpack(packed).astype(BF16)
            state[b * 4 + pr, :, 128:] = wide.astype(BF16)

    loop(4, enter)

    ones = jnp.ones((256, 128), BF16)

    def attend(i):
        b, pr, rows, cols = place(i)
        q, k, v = feat[0, rows, cols], feat[1, rows, cols], val[rows, cols]
        scores = mm(two(q), k, "NT")
        m = mask[b]
        low = jnp.concatenate([scores[:256] * m, scores[256:] * m], axis=0).astype(BF16)
        both = mm(low, jnp.concatenate([v, ones], axis=1))
        carried = mm(q, state[i])
        c = carry_on[b]
        numer = pick(both[:, :128]) + c * carried[:, :128]
        denom = pick(both[:, 128:]) + c * carried[:, 128:]
        inverse = 1.0 / denom
        result = numer * inverse
        den_inv[rows, cols] = inverse
        attn_wide[rows, cols] = result
        attn[rows, cols] = result.astype(BF16)

    loop(8, attend)
    forward_x(1)
    forward_x(2)
    weights_ready(1)

    work[...] = mm(attn[...], w_o[...])

    def mid_step(r):
        middle[r, :] = xin[r, :].astype(F32) + work[r, :]

    rows_loop(512, 64, mid_step)
    norm_rows(
        lambda r: middle[r, :].astype(BF16).astype(F32), gain_two, unit_two, rstd_two, normed_two
    )
    forward_y(3)
    weights_ready(2)
    for copy in og_copies:
        copy.wait_recv()
    own_og.wait()
    forward_x(3)
    weights_ready(3)

    def zero_rows(r):
        ffn[r, :] = jnp.zeros((64, 512), F32)
        norm_grad[r, :] = jnp.zeros((64, 512), F32)

    rows_loop(512, 64, zero_rows)

    def feed(i):
        jy = lax.rem(1 - hy + lax.div(i, 2), 2)
        jc = lax.rem(1 - hc + lax.rem(i, 2), 2)
        j = 2 * jy + jc
        work[...] = mm(normed_two[...], w_u[j])
        work_two[...] = mm(ogs[...], w_d[j], "NT")

        def step(r):
            v = work[r, :]
            sigma = 1.0 / (1.0 + jnp.exp(-v))
            hid[r, :] = (v * sigma).astype(BF16)
            hid_grad[r, :] = (work_two[r, :] * (sigma * (1.0 + v * (1.0 - sigma)))).astype(BF16)

        rows_loop(512, 64, step)
        part[0, jy, jc] = mm(hid[...], ogs[...], "TN").astype(BF16)
        part[1, jy, jc] = mm(normed_two[...], hid_grad[...], "TN").astype(BF16)
        ffn[...] += mm(hid[...], w_d[j])
        norm_grad[...] += mm(hid_grad[...], w_u[j], "NT")

    loop(4, feed)

    rpz = max(16, 256 // pairs)
    lane_width = 256 * 512 // pairs // rpz
    per_row = 512 // lane_width

    def piece(index):
        row = lax.div(index, per_row) * rpz
        return (
            pl.ds(pl.multiple_of(par * 256 + row, 16), rpz),
            pl.ds(pl.multiple_of(lax.rem(index, per_row) * lane_width, 128), lane_width),
        )

    def start_core(u):
        return [
            start(remote(part.at[u, jy, 1 - hc], buf_core.at[u, jy], core))
            for jy in (1 - hy, hy)
        ]

    def add_core(u, jy):
        def step(r):
            part[u, jy, hc, r, :] = (
                part[u, jy, hc, r, :].astype(F32) + buf_core[u, jy, r, :].astype(F32)
            ).astype(BF16)

        rows_loop(512, 128, step)

    def start_y(u):
        return start(remote(part.at[u, 1 - hy, hc], buf_y.at[u], ypeer))

    def add_y(u):
        def step(r):
            part[u, hy, hc, r, :] = (
                part[u, hy, hc, r, :].astype(F32) + buf_y[u, r, :].astype(F32)
            ).astype(BF16)

        rows_loop(512, 128, step)

    def start_x(u):
        rows = pl.ds(pl.multiple_of((1 - par) * 256, 256), 256)
        return start(remote(part.at[u, hy, hc, rows], buf_x.at[u], xpeer))

    def add_x(u):
        def step(r):
            rows = pl.ds(pl.multiple_of(par * 256 + r.start, 64), 64)
            part[u, hy, hc, rows, :] = (
                part[u, hy, hc, rows, :].astype(F32) + buf_x[u, r, :].astype(F32)
            ).astype(BF16)

        rows_loop(256, 64, step)

    def start_ring(u):
        copies = []
        for d in range(1, pairs):
            to, device = ring(d)
            rows, cols = piece(to)
            copies.append(
                start(remote(part.at[u, hy, hc, rows, cols], buf_ring.at[u, d - 1], device))
            )
        return copies

    def add_ring(u):
        rows, cols = piece(pair)
        total = part[u, hy, hc, rows, cols].astype(F32)
        for d in range(1, pairs):
            total = total + buf_ring[u, d - 1].astype(F32)
        own_piece[u] = total.astype(BF16)

    def start_spread(u):
        rows, cols = piece(pair)
        copies = [
            start(remote(own_piece.at[u], fin.at[u, rows, cols], ring(d)[1]))
            for d in range(1, pairs)
        ]
        return copies, local(own_piece.at[u], fin.at[u, rows, cols])

    def start_back(u):
        return start(remote(fin.at[u, half256], fin.at[u, half256], xpeer))

    core_copies = {0: start_core(0), 1: start_core(1)}

    gain_part[0] = jnp.zeros((8, 512), F32)
    row_512 = lax.broadcasted_iota(jnp.int32, (8, 512), 0)

    def norm_back(grad_ref, gain, unit_ref, rstd_ref, base, sink, row):
        def step(r):
            grad = grad_ref[r, :]
            unit = unit_ref[r, :]
            scaled = grad * gain[...]
            mean_one = jnp.mean(scaled, axis=-1, keepdims=True)
            mean_two = jnp.mean(scaled * unit, axis=-1, keepdims=True)
            rstd = rstd_ref[r, :]
            rstd = jnp.concatenate([rstd] * 4, axis=1)
            sink(r, base(r) + rstd * (scaled - mean_one - unit * mean_two))
            total = jnp.sum(grad * unit, axis=0, keepdims=True)
            gain_part[0] = gain_part[0] + jnp.where(row_512 == row, total, 0.0)

        rows_loop(512, 64, step)

    def sink_middle(r, grad):
        middle_grad[r, :] = grad
        middle_low[r, :] = grad.astype(BF16)
        lo_s[r, :] = (middle[r, :] + ffn[r, :]).astype(BF16)

    norm_back(
        norm_grad, gain_two, unit_two, rstd_two, lambda r: ogs[r, :].astype(F32), sink_middle, 1
    )

    y_copies = {}
    for u in (0, 1):
        core_copies[u][0].wait_recv()
        add_core(u, 1 - hy)
        y_copies[u] = start_y(u)
        core_copies[u][1].wait_recv()
        add_core(u, hy)

    def out_weight(j):
        part[2, lax.div(j, 2), lax.rem(j, 2), pl.ds(384, 128), :] = mm(
            attn[:, at128(j)], middle_low[...], "TN"
        ).astype(BF16)

    loop(4, out_weight)
    work[...] = mm(middle_low[...], w_o[...], "NT")

    head_ones = jnp.where(spread, 1.0, 0.0).astype(BF16)
    head_ones = jnp.concatenate([head_ones, head_ones], axis=0)
    first_lane = lax.rem(lane, 64) == 0
    second_lane = lax.rem(lane, 64) == 1

    def split(wide):
        high = wide.astype(BF16)
        return high, (wide - high.astype(F32)).astype(BF16)

    grad_z[...] = jnp.zeros_like(grad_z)

    def outer(i):
        b, pr, rows, cols = place(i)
        grad, inverse = work[rows, cols], den_inv[rows, cols]
        gnum = (grad * inverse).astype(BF16)
        high, low = split(grad * attn_wide[rows, cols])
        gden = -mm(jnp.concatenate([high, low], axis=1), head_ones) * inverse
        dhigh = gden.astype(BF16).astype(F32)
        num_grad[rows, cols] = gnum
        den_grad[rows, cols] = jnp.where(
            first_lane, dhigh, jnp.where(second_lane, gden - dhigh, 0.0)
        ).astype(BF16)
        queries = feat[0, rows, cols].astype(F32) * carry_on[b]
        grad_s[b, packed_rows(pr), :] = pack(mm(queries.astype(BF16), gnum, "TN"))
        grad_z[b, pl.ds(pr, 1), :] = jnp.sum(queries * gden, axis=0, keepdims=True)

    loop(8, outer)
    msg_gs[...] = (grad_s[0] + keep_first * grad_s[1]).astype(BF16)
    msg_gz[...] = jnp.where(row8 == 4, keep_first * keep_mid, grad_z[0] + keep_first * grad_z[1])
    backward = [shift(-d, msg_gs, msg_gz, buf_gs, buf_gz, d - 1) for d in (1, 2)]
    for d, copies in zip((1, 2), backward):

        @pl.when(pair >= d)
        def _():
            for copy in copies:
                copy.start()

    marks = jnp.where(first_lane | second_lane, 1.0, 0.0).astype(BF16)
    marks = jnp.broadcast_to(marks, (256, 128))

    def inner(i):
        b, pr, rows, cols = place(i)
        q, k, v = feat[0, rows, cols], feat[1, rows, cols], val[rows, cols]
        gnum, gden = num_grad[rows, cols], den_grad[rows, cols]
        q_two, gnum_two = two(q), two(gnum)
        grads = jnp.concatenate([gnum_two, two(gden)], axis=1)
        values = jnp.concatenate([v, marks], axis=1)
        m, mt = mask[b], mask_t[b]
        gsc = mm(grads, values, "NT")
        gsc = jnp.concatenate([gsc[:256] * m, gsc[256:] * m], axis=0).astype(BF16)
        qgrad = pick(mm(gsc, k)) + carry_on[b] * mm(
            jnp.concatenate([gnum, gden], axis=1), state[i], "NT"
        )
        low_grads[0, rows, cols] = (qgrad * jnp.minimum(q.astype(F32), 1.0)).astype(BF16)
        gsc_t = mm(values, grads, "NT")
        gsc_t = jnp.concatenate([gsc_t[:, :256] * mt, gsc_t[:, 256:] * mt], axis=1).astype(BF16)
        key_acc[rows, cols] = mm(gsc_t, q_two)
        sc_t = mm(k, q_two, "NT")
        sc_t = jnp.concatenate([sc_t[:, :256] * mt, sc_t[:, 256:] * mt], axis=1).astype(BF16)
        val_acc[rows, cols] = mm(sc_t, gnum_two)

    loop(8, inner)

    x_copies = {}
    for u in (0, 1):
        y_copies[u].wait_recv()
        add_y(u)
        x_copies[u] = start_x(u)

    for d, copies in zip((1, 2), backward):

        @pl.when(pair + d < pairs)
        def _():
            for copy in copies:
                copy.wait_recv()

    pass_on = buf_gz[0, pl.ds(4, 1), :]
    buf_gz[0] = buf_gz[0] + pass_on * buf_gz[1]

    def leave(i):
        b, pr, rows, cols = place(i)
        leaving = buf_gs[0, packed_rows(pr), :].astype(F32) + pass_on * buf_gs[
            1, packed_rows(pr), :
        ].astype(F32)
        z_leaving = buf_gz[0, pl.ds(pr, 1), :]
        first_block = (1 - b).astype(F32)
        scale = first_block * keep_mid + (1.0 - first_block)
        leaving = scale * leaving + first_block * grad_s[1, packed_rows(pr), :]
        z_leaving = scale * z_leaving + first_block * grad_z[1, pl.ds(pr, 1), :]
        square = unpack(leaving).astype(BF16)
        k, v = feat[1, rows, cols], val[rows, cols]
        tail = seg_col[b] == seg_col[b, pl.ds(255, 1), :]
        kgrad = key_acc[rows, cols] + jnp.where(tail, mm(v, square, "NT") + z_leaving, 0.0)
        low_grads[1, rows, cols] = (kgrad * jnp.minimum(k.astype(F32), 1.0)).astype(BF16)
        vgrad = val_acc[rows, cols] + jnp.where(tail, mm(k, square), 0.0)
        low_grads[2, rows, cols] = vgrad.astype(BF16)

    loop(8, leave)

    def qkv_weight(n):
        j, i = lax.div(n, 3), lax.rem(n, 3)
        part[2, lax.div(j, 2), lax.rem(j, 2), at128(i), :] = mm(
            low_grads[i, :, at128(j)], normed[...], "TN"
        ).astype(BF16)

    loop(12, qkv_weight)
    core_copies[2] = start_core(2)

    norm_grad[...] = mm(low_grads[0], w_qkv[0], "NT")
    norm_grad[...] += mm(low_grads[1], w_qkv[1], "NT")
    norm_grad[...] += mm(low_grads[2], w_qkv[2], "NT")

    core_copies[2][0].wait_recv()
    add_core(2, 1 - hy)
    y_copies[2] = start_y(2)
    core_copies[2][1].wait_recv()
    add_core(2, hy)

    def sink_input(r, grad):
        ig_s[r, :] = grad.astype(BF16)

    norm_back(norm_grad, gain_one, unit_one, rstd_one, lambda r: middle_grad[r, :], sink_input, 0)
    lo_copies, lo_own = scatter_out(lo_s, lo_out)
    ig_copies, ig_own = scatter_out(ig_s, ig_out)

    ring_copies, spread_copies, back_copies = {}, {}, {}

    def x_done(u):
        x_copies[u].wait_recv()
        add_x(u)
        ring_copies[u] = start_ring(u)

    def ring_done(u):
        for copy in ring_copies[u]:
            copy.wait_recv()
        add_ring(u)
        spread_copies[u] = start_spread(u)

    def spread_done(u):
        for copy in spread_copies[u][0]:
            copy.wait_recv()
        spread_copies[u][1].wait()
        back_copies[u] = start_back(u)

    def gain_stage(n, device):
        copy = start(remote(gain_part.at[n], gain_buf.at[n], device))
        copy.wait_recv()
        gain_part[n + 1] = gain_part[n] + gain_buf[n]

    x_done(0)
    gain_stage(0, core)
    x_done(1)
    gain_stage(1, ypeer)
    ring_done(0)
    gain_stage(2, xpeer)
    y_copies[2].wait_recv()
    add_y(2)
    x_copies[2] = start_x(2)
    ring_done(1)
    gain_copies = [
        start(remote(gain_part.at[3], gain_buf.at[2 + d], ring(d)[1])) for d in range(1, pairs)
    ]
    spread_done(0)
    x_done(2)
    spread_done(1)
    for copy in gain_copies:
        copy.wait_recv()
    total = gain_part[3]
    for d in range(1, pairs):
        total = total + gain_buf[2 + d]
    gain_part[4] = total
    gains[...] = gain_part[4, :, hcol]
    ring_done(2)
    spread_done(2)

    for u in range(UNITS):
        back_copies[u].wait_recv()
    for copy in lo_copies + ig_copies:
        copy.wait_recv()
    lo_own.wait()
    ig_own.wait()
    for copy in sends:
        copy.wait_send()
    for d in (1, 2):

        @pl.when(pair + d < pairs)
        def _():
            for copy in forward[d - 1]:
                copy.wait_send()

        @pl.when(pair >= d)
        def _():
            for copy in backward[d - 1]:
                copy.wait_send()


def widen_kernel(ig, fin, ig_o, q_o, k_o, v_o, o_o, u_o, d_o):
    ig_o[...] = ig[...].astype(F32)
    d_o[...] = fin[0].astype(F32)
    u_o[...] = fin[1].astype(F32)
    for i, out in enumerate((q_o, k_o, v_o)):
        out[...] = fin[2, i * 128 : (i + 1) * 128].astype(F32).T
    o_o[...] = fin[2, 384:].astype(F32)


def body(
    tokens,
    norm_gain,
    query_weight,
    key_weight,
    value_weight,
    attention_output_weight,
    feedforward_norm_gain,
    up_weight,
    down_weight,
    segment_ids,
    out_grad,
):
    batch, length, share = tokens.shape
    width, head_cols = query_weight.shape
    units = up_weight.shape[1]
    pairs = lax.axis_size("seq") // 2
    assert lax.axis_size("head") == 4 and batch == 8 and length == BLOCK
    assert (width, share, head_cols, units) == (512, 128, 128, 512)
    others = pairs - 1
    rpz = max(16, 256 // pairs)
    lane_width = 256 * 512 // pairs // rpz
    anywhere = pl.BlockSpec(memory_space=pl.ANY)
    vmem = pl.BlockSpec(memory_space=pltpu.VMEM)
    copies = 7 * 4 + 1 + 5 * KINDS + 8 + UNITS * (5 + 2 * others) + 3 + others
    scratch = [
        pltpu.VMEM((512, 512), BF16),
        pltpu.VMEM((512, 512), BF16),
        pltpu.VMEM((3, 512, 512), BF16),
        pltpu.VMEM((512, 512), BF16),
        pltpu.VMEM((4, 512, 512), BF16),
        pltpu.VMEM((4, 512, 512), BF16),
        pltpu.VMEM((8, 256), jnp.int32),
        pltpu.VMEM((512, 512), F32),
        pltpu.VMEM((512, 512), F32),
        pltpu.VMEM((512, 128), F32),
        pltpu.VMEM((512, 128), F32),
        pltpu.VMEM((512, 512), BF16),
        pltpu.VMEM((512, 512), BF16),
        pltpu.VMEM((2, 512, 512), BF16),
        pltpu.VMEM((512, 512), BF16),
        pltpu.VMEM((2, 256, 256), F32),
        pltpu.VMEM((2, 256, 256), F32),
        pltpu.VMEM((2, 256, 128), F32),
        pltpu.VMEM((2, 256, 128), F32),
        pltpu.VMEM((2, 256, 128), F32),
        pltpu.VMEM((2, 8, 128), F32),
        pltpu.VMEM((256, 128), BF16),
        pltpu.VMEM((8, 128), F32),
        pltpu.VMEM((2, 256, 128), BF16),
        pltpu.VMEM((2, 8, 128), F32),
        pltpu.VMEM((8, 128, 256), BF16),
        pltpu.VMEM((512, 512), BF16),
        pltpu.VMEM((512, 512), F32),
        pltpu.VMEM((512, 512), F32),
        pltpu.VMEM((512, 512), F32),
        pltpu.VMEM((512, 512), F32),
        pltpu.VMEM((512, 512), F32),
        pltpu.VMEM((512, 512), BF16),
        pltpu.VMEM((512, 512), BF16),
        pltpu.VMEM((512, 512), F32),
        pltpu.VMEM((512, 512), F32),
        pltpu.VMEM((512, 512), F32),
        pltpu.VMEM((512, 512), BF16),
        pltpu.VMEM((512, 512), BF16),
        pltpu.VMEM((512, 512), BF16),
        pltpu.VMEM((2, 256, 128), F32),
        pltpu.VMEM((2, 8, 128), F32),
        pltpu.VMEM((256, 128), BF16),
        pltpu.VMEM((8, 128), F32),
        pltpu.VMEM((2, 256, 128), BF16),
        pltpu.VMEM((2, 8, 128), F32),
        pltpu.VMEM((512, 512), F32),
        pltpu.VMEM((512, 512), F32),
        pltpu.VMEM((3, 512, 512), BF16),
        pltpu.VMEM((512, 512), BF16),
        pltpu.VMEM((512, 512), BF16),
        pltpu.VMEM((UNITS, 2, 2, 512, 512), BF16),
        pltpu.VMEM((UNITS, 2, 512, 512), BF16),
        pltpu.VMEM((UNITS, 512, 512), BF16),
        pltpu.VMEM((UNITS, 256, 512), BF16),
        pltpu.VMEM((UNITS, others, rpz, lane_width), BF16),
        pltpu.VMEM((UNITS, rpz, lane_width), BF16),
        pltpu.VMEM((5, 8, 512), F32),
        pltpu.VMEM((3 + others, 8, 512), F32),
        pltpu.SemaphoreType.DMA((16,)),
        pltpu.SemaphoreType.DMA((copies,)),
        pltpu.SemaphoreType.DMA((copies,)),
    ]
    lo, ig, fin, gains = pl.pallas_call(
        functools.partial(layer_kernel, pairs),
        out_shape=(
            jax.ShapeDtypeStruct((batch, length, share), BF16),
            jax.ShapeDtypeStruct((batch, length, share), BF16),
            jax.ShapeDtypeStruct((UNITS, 512, 512), BF16),
            jax.ShapeDtypeStruct((8, 128), F32),
        ),
        in_specs=[anywhere] * 8 + [vmem] * 3,
        out_specs=(anywhere, anywhere, anywhere, vmem),
        scratch_shapes=scratch,
        compiler_params=pltpu.CompilerParams(
            collective_id=0, has_side_effects=True, vmem_limit_bytes=56 * MIB
        ),
        cost_estimate=pl.CostEstimate(
            flops=11 * 10**9, bytes_accessed=8 * MIB, transcendentals=4 * 10**6
        ),
        name="layer",
    )(
        tokens,
        out_grad,
        query_weight,
        key_weight,
        value_weight,
        attention_output_weight,
        up_weight,
        down_weight,
        segment_ids,
        norm_gain[None],
        feedforward_norm_gain[None],
    )
    wide = pl.pallas_call(
        widen_kernel,
        out_shape=(
            jax.ShapeDtypeStruct((batch, length, share), F32),
            jax.ShapeDtypeStruct((512, 128), F32),
            jax.ShapeDtypeStruct((512, 128), F32),
            jax.ShapeDtypeStruct((512, 128), F32),
            jax.ShapeDtypeStruct((128, 512), F32),
            jax.ShapeDtypeStruct((512, 512), F32),
            jax.ShapeDtypeStruct((512, 512), F32),
        ),
        in_specs=[vmem] * 2,
        out_specs=(vmem,) * 7,
        compiler_params=pltpu.CompilerParams(vmem_limit_bytes=32 * MIB),
        name="widen",
    )(ig, fin)
    ig_w, q_w, k_w, v_w, o_w, u_w, d_w = wide
    return (lo, ig_w, gains[0], q_w, k_w, v_w, o_w, gains[1], u_w, d_w)


def solution(mesh):
    in_specs = (
        P(None, "seq", "head"),
        P(),
        P(None, "head"),
        P(None, "head"),
        P(None, "head"),
        P("head", None),
        P(),
        P(None, "head"),
        P("head", None),
        P(None, "seq"),
        P(None, "seq", "head"),
    )
    out_specs = (
        P(None, "seq", "head"),
        P(None, "seq", "head"),
        P("head"),
        P(None, "head"),
        P(None, "head"),
        P(None, "head"),
        P("head", None),
        P("head"),
        P(None, "head"),
        P("head", None),
    )
    return jax.shard_map(body, mesh=mesh, in_specs=in_specs, out_specs=out_specs, check_vma=False)
```

time: 661 us -> 157 us (0.24); the launches traced: 653 us -> 157 us
  waiting for transfers between devices: 299 us -> 0 us
  Pallas kernels: 0 us -> 152 us
  blocking collectives: 150 us -> 0 us
  matrix products: 80.6 us -> 0 us
  other arithmetic: 66.9 us -> 0 us
  local copies, waits for them, and re-layouts: 39.8 us -> 4.52 us
  between operations: 15.8 us -> 0.66 us
    pallas_call x0 -> x2, Pallas kernels: none -> 152 us  [the longest x1 150 us: body(): pl.pallas_call(functools.partial(layer_kernel, pairs), out_shape=(jax.Sha...]
    reduce_scatter x3 -> x0, waiting for transfers between devices: 103 us -> none  [the longest x2 59.4 us: norm_back(): lax.psum_scatter(grad_part, 'head', scatter_dimension=2, tiled=True)]
    all_gather x6 -> x0, waiting for transfers between devices: 98 us -> none  [the longest x1 25.5 us: body(): whole_in = lax.all_gather(tokens, 'head', axis=2, tiled=True)]
    psum x1 -> x0, waiting for transfers between devices: 96.8 us -> none  [body(): lax.psum((query_weight_grad, key_weight_grad, value_weight_grad, out_weig...]
    dot_general x33 -> x0, matrix products: 80.6 us -> none  [the longest x1 5.25 us: body(): jnp.einsum('mtd,fd->mtf', grad_full, down_weight, preferred_element_type=...]
    all_gather x2 -> x0, blocking collectives: 62.3 us -> none  [the longest x1 31.3 us: carried_in(): lax.all_gather(part.astype(kind), axis)]
    psum x3 -> x0, blocking collectives: 44.1 us -> none  [the longest x1 22.3 us: body(): lax.psum((query_weight_grad, key_weight_grad, value_weight_grad, out_weig...]
    unnamed x2 -> x0, blocking collectives: 43.4 us -> none
  transfers between devices with their start and end apart: 11 -> 0, of which waited for: 9 -> 0; matrix products, arithmetic and copies ran while one was open for 17% -> 0% of each run, Pallas kernels for 0% -> 0%
where the time goes in v1:
time: 157 us
  Pallas kernels  152 us (97%)
  local copies, waits for them, and re-layouts  4.52 us (3%)
    pallas_call x1, Pallas kernels, body(): pl.pallas_call(functools.partial(layer_kernel, pairs), out_shape=(jax.Sha...  150 us
    unnamed x7, local copies, waits for them, and re-layouts  3.25 us

profile of v1, /device:TPU:0, one launch (start us, length us, event | category | flops | bytes accessed | tf_op | source)
XLA Modules:
  0.0 156.9 jit_solution(1868506708222725068)
XLA Ops:
  0.6 149.7 %layer.1 = (bf16[8,256,128]{2,1,0:T(8,128)(2,1)}, bf16[8,256,128]{2,1,0:T(8,128)(2,1)}, bf16[3,512,512]{2,1,0:T(8,128)(2,1)}, f32[8,128]{1,0:T(8,128)}) custom-call(bf16[8,256,128]{2,1,0:T(8,128)(2,1)} %tok.1, bf16[8,256,128]{2,1,0:T(8,128)(2,1)} %og_in.1, bf16[512,128]{1,0:T(8,128)(2,1)} %wq.1, bf16[512,128]{1,0:T(8,128)(2,1)} %wk.1, bf16[512,128]{1,0:T(8,128)(2,1)} %wv.1, ...), custom_call_target="tpu_custom_call" | custom-call | flops 11000000512 | bytes 8388608 | tf_op jit(solution)/shard_map/layer/pallas_call | solution.py:926
  150.3 1.3 slice_bitcast_fusion
  151.6 0.0 copy-start
  151.6 1.4 copy-done
  153.0 0.0 copy-start.1
  153.0 1.0 copy-done.1
  154.0 0.0 copy-start.2
  154.0 2.1 %widen.1 = (f32[8,256,128]{2,1,0:T(8,128)}, f32[512,128]{1,0:T(8,128)}, f32[512,128]{1,0:T(8,128)}, f32[512,128]{1,0:T(8,128)}, f32[128,512]{1,0:T(8,128)}, /*index=5*/f32[512,512]{1,0:T(8,128)}, f32[512,512]{1,0:T(8,128)}) custom-call(bf16[8,256,128]{2,1,0:T(8,128)(2,1)S(1)} %copy-done.1, bf16[3,512,512]{2,1,0:T(8,128)(2,1)S(1)} %copy-done), custom_call_target="tpu_custom_call" | custom-call | tf_op jit(solution)/shard_map/widen/pallas_call | solution.py:957
  156.1 0.0 copy-done.2
  156.2 0.8 copy.22
Async XLA Ops:
  151.6 1.4 copy-start
  153.0 1.0 copy-start.1
  154.0 2.1 %copy-start.2 = (bf16[8,256,128]{2,1,0:T(8,128)(2,1)S(1)}, bf16[8,256,128]{2,1,0:T(8,128)(2,1)}, u32[]{:S(2)}) copy-start(bf16[8,256,128]{2,1,0:T(8,128)(2,1)} %get-tuple-element.44) | copy-start | bytes 1572868

commit v2 on v1

v2 whole, which is shorter than its diff:
```python
import functools
from types import SimpleNamespace

import jax
import jax.numpy as jnp
from jax import lax
from jax.experimental import pallas as pl
from jax.experimental.pallas import tpu as pltpu
from jax.sharding import PartitionSpec as P

DH = 64
BLOCK = 256
EPSILON = 1e-05
MESH = pl.DeviceIdType.MESH
F32 = jnp.float32
BF16 = jnp.bfloat16
MIB = 1 << 20
KINDS = 4
OWNERS = 4
CHUNKS = (
    (0, 0, 512, 0, 256, True),
    (0, 0, 512, 256, 256, True),
    (1, 0, 512, 0, 256, False),
    (1, 0, 512, 256, 256, False),
    (2, 384, 128, 0, 512, True),
    (2, 0, 384, 0, 256, True),
    (2, 0, 384, 256, 256, False),
)
COMBOS = ((0, 1, 0), (0, 1, 1), (1, 1, 0), (1, 1, 1), (1, 0, 0), (1, 0, 1), (0, 0, 1))


def mm(left, right, form="NN"):
    dims = {"NN": ((1,), (0,)), "NT": ((1,), (1,)), "TN": ((0,), (0,))}[form]
    return lax.dot_general(left, right, (dims, ((), ())), preferred_element_type=F32)


def loop(count, step):
    def run(i, carry):
        step(i)
        return carry

    lax.fori_loop(0, count, run, 0)


def span(start, size, multiple=None):
    return pl.ds(pl.multiple_of(start, multiple or size), size)


def rows_loop(total, chunk, step):
    loop(total // chunk, lambda i: step(span(i * chunk, chunk)))


def at128(i):
    return span(i * 128, 128)


def layer_kernel(pairs, names, *refs):
    (tok, og_in, wq, wk, wv, wo, wu, wd, seg, gain_one, gain_two) = refs[:11]
    (lo_out, ig_out, fin, gains) = refs[11:15]
    r_ = SimpleNamespace(**dict(zip(names, refs[15:])))
    chunk_refs = refs[15 + len(names) : -3]
    local_sem, send_sem, recv_sem = refs[-3:]
    xin, ogs, w_qkv, w_o, w_u = (
        r_.xin, r_.ogs, r_.w_qkv, r_.w_o, r_.w_u,
    )
    w_d, unit_one, unit_two, rstd_one, rstd_two = (
        r_.w_d, r_.unit_one, r_.unit_two, r_.rstd_one, r_.rstd_two,
    )
    normed, normed_two, feat, val, mask = (
        r_.normed, r_.normed_two, r_.feat, r_.val, r_.mask,
    )
    seg_col, carry_on, state, scores_low, own_s = (
        r_.seg_col, r_.carry_on, r_.state, r_.scores_low, r_.own_s,
    )
    own_z, msg_s, msg_z, buf_s, buf_z = (
        r_.own_z, r_.msg_s, r_.msg_z, r_.buf_s, r_.buf_z,
    )
    grad_s, grad_z, msg_gs, msg_gz, buf_gs = (
        r_.grad_s, r_.grad_z, r_.msg_gs, r_.msg_gz, r_.buf_gs,
    )
    buf_gz, attn, attn_wide, den_inv, middle = (
        r_.buf_gz, r_.attn, r_.attn_wide, r_.den_inv, r_.middle,
    )
    work, work_two, hid, hid_grad, ffn = (
        r_.work, r_.work_two, r_.hid, r_.hid_grad, r_.ffn,
    )
    norm_grad, middle_grad, middle_low, num_grad, den_grad = (
        r_.norm_grad, r_.middle_grad, r_.middle_low, r_.num_grad, r_.den_grad,
    )
    key_acc, val_acc, low_grads, lo_s, ig_s = (
        r_.key_acc, r_.val_acc, r_.low_grads, r_.lo_s, r_.ig_s,
    )
    part, buf_core, gain_part, gain_buf, seg_other = (
        r_.part, r_.buf_core, r_.gain_part, r_.gain_buf, r_.seg_other,
    )

    s = lax.axis_index("seq")
    h = lax.axis_index("head")
    pair, par = lax.div(s, 2), lax.rem(s, 2)
    hy, hc = lax.div(h, 2), lax.rem(h, 2)
    member = par * 4 + h
    zb = lax.rem(pair, 2)

    counter = [0]
    sends = []
    local_ids = iter(range(1000))

    def take(n=1):
        counter[0] += n
        return counter[0] - n

    def guarded(cond, act):
        if cond is None:
            act()
        else:
            pl.when(cond)(act)

    def peer(dp, dy, dc):
        return (1 - par if dp else par, 1 - hy if dy else hy, 1 - hc if dc else hc)

    def address(par_to, y_to, c_to):
        return (2 * pair + par_to, 2 * y_to + c_to)

    core, ypeer, xpeer = (address(*peer(*d)) for d in ((0, 0, 1), (0, 1, 0), (1, 0, 0)))
    zpeer = (2 * (pair + 1 - 2 * zb) + par, h)

    def ring(d):
        to = lax.rem(pair + d, pairs)
        return to, (2 * to + par, h)

    def remote(src, dst, device, i=None):
        i = take() if i is None else i
        return pltpu.make_async_remote_copy(
            src_ref=src,
            dst_ref=dst,
            send_sem=send_sem.at[i],
            recv_sem=recv_sem.at[i],
            device_id=device,
            device_id_type=MESH,
        )

    def start(copy):
        copy.start()
        sends.append(copy)
        return copy

    def send(src, dst, device):
        return start(remote(src, dst, device))

    def local(src, dst):
        copy = pltpu.make_async_copy(src, dst, local_sem.at[next(local_ids)])
        copy.start()
        return copy

    def each_ring(act):
        if pairs <= 4:
            for d in range(1, pairs):
                act(d)
        else:
            loop(pairs - 1, lambda i: act(i + 1))

    hcol = at128(h)
    half256 = span(par * 256, 256)
    own_w = [
        [local(w, w_qkv.at[i, :, hcol]) for i, w in enumerate((wq, wk, wv))],
        [local(wo, w_o.at[hcol])],
        [local(wu, w_u.at[h])],
        [local(wd, w_d.at[h])],
    ]
    own_tok = local(tok.at[member], xin.at[half256, hcol])
    own_og = local(og_in.at[member], ogs.at[half256, hcol])
    row8 = lax.broadcasted_iota(jnp.int32, (8, 128), 0)
    neutral = jnp.where(row8 == 4, -1.0, 0.0).astype(F32)
    for slot in range(2):
        buf_s[slot] = jnp.zeros((256, 128), BF16)
        buf_gs[slot] = jnp.zeros((256, 128), BF16)
        buf_gz[slot] = jnp.zeros((8, 128), F32)
        for order in range(2):
            buf_z[slot, order] = neutral

    barrier = pltpu.get_barrier_semaphore()
    for d in COMBOS:
        pl.semaphore_signal(barrier, inc=1, device_id=address(*peer(*d)), device_id_type=MESH)
    each_ring(
        lambda d: pl.semaphore_signal(
            barrier, inc=1, device_id=ring(d)[1], device_id_type=MESH
        )
    )
    pl.semaphore_wait(barrier, len(COMBOS) + pairs - 1)

    def scatter_in(src, dst):
        copies = []
        for d in COMBOS:
            par_to, y_to, c_to = peer(*d)
            copies.append(
                send(
                    src.at[par_to * 4 + 2 * y_to + c_to],
                    dst.at[half256, hcol],
                    address(par_to, y_to, c_to),
                )
            )
        return copies

    def scatter_out(src, dst):
        copies = []
        for d in COMBOS:
            par_to, y_to, c_to = peer(*d)
            copies.append(
                send(
                    src.at[span(par_to * 256, 256), at128(2 * y_to + c_to)],
                    dst.at[member],
                    address(par_to, y_to, c_to),
                )
            )
        return copies, local(src.at[half256, hcol], dst.at[member])

    across = 2 * (1 - hy) + hc
    quarter = par + 2 * zb
    quarter_x = 1 - par + 2 * zb
    quarter_z = par + 2 * (1 - zb)
    quarter_far = 1 - par + 2 * (1 - zb)

    def view(kind, shard, eighth=None, eighths=2):
        rows = 32 if kind == 1 else 128
        unit = rows // 2
        if kind == 0:
            where = slice(None) if eighth is None else span(eighth * unit, unit * eighths, unit)
            return w_qkv.at[:, where, at128(shard)]
        if kind == 1:
            if eighth is None:
                return w_o.at[at128(shard)]
            return w_o.at[span(shard * 128 + eighth * unit, unit * eighths, unit)]
        ref = w_u if kind == 2 else w_d
        if eighth is None:
            return ref.at[shard]
        return ref.at[shard, span(eighth * unit, unit * eighths, unit)]

    wt = {}

    def pass_on_weight(kind, eighth, eighths, device, shard=None):
        ref = view(kind, across if shard is None else shard, eighth, eighths)
        return send(ref, ref, device)

    def weight_y(kind):
        wt[kind, "y"] = pass_on_weight(kind, 2 * quarter, 2, ypeer, h)

    def weight_core(kind):
        own = view(kind, h)
        wt[kind, "c"] = [send(own, own, core)]

    def weight_near(kind):
        wt[kind, "y"].wait_recv()
        wt[kind, "x"] = pass_on_weight(kind, 2 * quarter, 2, xpeer)
        wt[kind, "z"] = pass_on_weight(kind, 2 * quarter, 2, zpeer)
        wt[kind, "c"].append(pass_on_weight(kind, 2 * quarter, 2, core))

    def weight_far(kind):
        wt[kind, "x"].wait_recv()
        wt[kind, "z2"] = pass_on_weight(kind, 2 * quarter_x, 1, zpeer)
        wt[kind, "c"].append(pass_on_weight(kind, 2 * quarter_x, 2, core))
        wt[kind, "z"].wait_recv()
        wt[kind, "x2"] = pass_on_weight(kind, 2 * quarter_z + 1, 1, xpeer)
        wt[kind, "c"].append(pass_on_weight(kind, 2 * quarter_z, 2, core))

    def weight_last(kind):
        wt[kind, "z2"].wait_recv()
        wt[kind, "x2"].wait_recv()
        wt[kind, "c"].append(pass_on_weight(kind, 2 * quarter_far, 2, core))

    def weight_own(kind):
        wt[kind, "c"][0].wait_recv()

    def weight_ready(kind):
        for copy in wt[kind, "c"][1:]:
            copy.wait_recv()

    for copy in own_w[0]:
        copy.wait()
    weight_y(0)
    tokens_in = scatter_in(tok, xin)
    seg_copy = send(seg, seg_other, xpeer)
    weight_core(0)
    for kind in (1, 2, 3):
        for copy in own_w[kind]:
            copy.wait()
        weight_core(kind)
    weight_near(0)
    for copy in tokens_in:
        copy.wait_recv()
    own_tok.wait()
    for kind in (1, 2, 3):
        weight_y(kind)

    def norm_rows(source, gain, unit_ref, rstd_ref, out_ref):
        def step(r):
            x = source(r)
            center = x - jnp.mean(x, axis=-1, keepdims=True)
            scale = lax.rsqrt(jnp.mean(center * center, axis=-1, keepdims=True) + EPSILON)
            unit = center * scale
            unit_ref[r, :] = unit
            rstd_ref[r, :] = jnp.broadcast_to(scale, (unit.shape[0], 128))
            out_ref[r, :] = (unit * gain[...]).astype(BF16)

        rows_loop(512, 64, step)

    norm_rows(lambda r: xin[r, :].astype(F32), gain_one, unit_one, rstd_one, normed)

    seg_copy.wait_recv()
    own_row = seg[pl.ds(member, 1), :]
    other_row = seg_other[pl.ds(member, 1), :]
    seg_rows = (
        (own_row * (1 - par) + other_row * par).astype(F32),
        (own_row * par + other_row * (1 - par)).astype(F32),
    )
    first = lax.broadcasted_iota(jnp.int32, (256, 256), 0)
    second = lax.broadcasted_iota(jnp.int32, (256, 256), 1)
    for b in range(2):
        along = jnp.broadcast_to(seg_rows[b], (256, 256))
        down = along.T
        mask[b] = jnp.where((along == down) & (second <= first), 1.0, 0.0)
        seg_col[b] = down[:, :128]
    weight_far(0)
    weight_own(0)

    lane = lax.broadcasted_iota(jnp.int32, (1, 128), 1)
    low_lanes = lane < 64
    spread = (
        lax.broadcasted_iota(jnp.int32, (128, 128), 0) // 64
        == lax.broadcasted_iota(jnp.int32, (128, 128), 1) // 64
    )

    def place(i):
        b, pr = lax.div(i, 4), lax.rem(i, 4)
        return b, pr, span(b * 256, 256), at128(pr)

    def side_place(i, side):
        return place(lax.div(i, 2) * 4 + 2 * side + lax.rem(i, 2))

    def pack(square):
        return jnp.where(low_lanes, square[:64], square[64:])

    def two(rows):
        zero = jnp.zeros_like(rows)
        return jnp.concatenate(
            [jnp.where(low_lanes, rows, zero), jnp.where(low_lanes, zero, rows)], axis=0
        )

    def pick(stacked):
        return jnp.where(low_lanes, stacked[:256], stacked[256:])

    def packed_rows(pr):
        return span(pr * 64, 64)

    last_rows = [seg_col[b, pl.ds(255, 1), :] for b in range(2)]
    keep_mid = jnp.where(last_rows[0] >= last_rows[1], 1.0, 0.0)

    def project(side):
        cols = span(side * 256, 256)

        def step_kind(i):
            work[:, :256] = mm(normed[...], w_qkv[i, :, cols])

            def step(r):
                v = work[r, :256]
                feat[i, r, cols] = jnp.where(
                    v > 0, v + 1.0, jnp.exp(jnp.minimum(v, 0.0))
                ).astype(BF16)

            rows_loop(512, 64, step)

        loop(2, step_kind)
        val[:, cols] = mm(normed[...], w_qkv[2, :, cols]).astype(BF16)

    def own_state(i, side):
        b, pr, rows, cols = side_place(i, side)
        tail = seg_col[b] == seg_col[b, pl.ds(255, 1), :]
        keys = feat[1, rows, cols].astype(F32)
        keys = jnp.where(tail, keys, 0.0)
        own_s[b, packed_rows(pr), :] = pack(mm(keys.astype(BF16), val[rows, cols], "TN"))
        own_z[b, pl.ds(pr, 1), :] = jnp.sum(keys, axis=0, keepdims=True)

    def shift(d, pieces, base):
        to = lax.rem(pair + d + pairs, pairs)
        device = (2 * to + par, h)
        return [remote(src, dst, device, base + i) for i, (src, dst) in enumerate(pieces)]

    forward = {}

    def send_state(order, side):
        loop(4, lambda i: own_state(i, side))
        rows = span(side * 128, 128)
        msg_s[rows, :] = (own_s[1, rows, :] + keep_mid * own_s[0, rows, :]).astype(BF16)
        msg_z[order] = jnp.where(row8 == 4, last_rows[1], own_z[1] + keep_mid * own_z[0])
        for d in (1, 2):
            copies = shift(
                d,
                [
                    (msg_s.at[rows], buf_s.at[d - 1, rows]),
                    (msg_z.at[order], buf_z.at[d - 1, order]),
                ],
                take(2),
            )
            forward[order, d] = copies

            @pl.when(pair + d < pairs)
            def _():
                for copy in copies:
                    copy.start()

    own_z[...] = jnp.zeros_like(own_z)
    project(hy)
    send_state(0, hy)
    weight_last(0)
    og_copies = scatter_in(og_in, ogs)
    weight_near(1)
    weight_ready(0)
    project(1 - hy)
    send_state(1, 1 - hy)
    weight_near(2)
    weight_near(3)
    weight_far(1)

    ones = jnp.ones((256, 128), BF16)
    ready = {}

    def receive_state(order):
        for d in (1, 2):

            @pl.when(pair >= d)
            def _():
                for copy in forward[order, d]:
                    copy.wait_recv()

        if order == 0:
            last_in = buf_z[0, 0, pl.ds(4, 1), :]
            ready["keep_in"] = jnp.where(buf_z[1, 0, pl.ds(4, 1), :] >= last_in, 1.0, 0.0)
            ready["keep_first"] = jnp.where(last_in >= last_rows[0], 1.0, 0.0)
            carry_on[0] = jnp.where(seg_col[0] == last_in, 1.0, 0.0)
            carry_on[1] = jnp.where(seg_col[1] == last_rows[0], 1.0, 0.0)
        buf_z[0, order] = buf_z[0, order] + ready["keep_in"] * buf_z[1, order]

    def enter(order, side):
        def step(i):
            pr = 2 * side + i
            entering = buf_s[0, packed_rows(pr), :].astype(F32) + ready["keep_in"] * buf_s[
                1, packed_rows(pr), :
            ].astype(F32)
            z_in = buf_z[0, order, pl.ds(pr, 1), :]
            middle_s = own_s[0, packed_rows(pr), :] + ready["keep_first"] * entering
            middle_z = own_z[0, pl.ds(pr, 1), :] + ready["keep_first"] * z_in
            for b, (packed, z_row) in enumerate(((entering, z_in), (middle_s, middle_z))):
                wide = jnp.where(spread, jnp.broadcast_to(z_row, (128, 128)).T, 0.0)
                state[b * 4 + pr, :, :128] = two(packed).astype(BF16)
                state[b * 4 + pr, :, 128:] = wide.astype(BF16)

        loop(2, step)

    def attend(i, side):
        b, pr, rows, cols = side_place(i, side)
        q, k, v = feat[0, rows, cols], feat[1, rows, cols], val[rows, cols]
        scores = mm(two(q), k, "NT")
        m = mask[b]
        low = jnp.concatenate([scores[:256] * m, scores[256:] * m], axis=0).astype(BF16)
        scores_low[b * 4 + pr] = low
        both = mm(low, jnp.concatenate([v, ones], axis=1))
        carried = mm(q, state[b * 4 + pr])
        c = carry_on[b]
        numer = pick(both[:, :128]) + c * carried[:, :128]
        denom = pick(both[:, 128:]) + c * carried[:, 128:]
        inverse = 1.0 / denom
        result = numer * inverse
        den_inv[rows, cols] = inverse
        attn_wide[rows, cols] = result
        attn[rows, cols] = result.astype(BF16)

    for order, side in ((0, hy), (1, 1 - hy)):
        receive_state(order)
        enter(order, side)
        loop(4, lambda i: attend(i, side))
        if order == 0:
            weight_last(1)
            weight_far(2)
    keep_first = ready["keep_first"]
    weight_far(3)
    weight_own(1)
    weight_ready(1)

    work[...] = mm(attn[...], w_o[...])

    def mid_step(r):
        middle[r, :] = xin[r, :].astype(F32) + work[r, :]

    rows_loop(512, 64, mid_step)
    norm_rows(
        lambda r: middle[r, :].astype(BF16).astype(F32), gain_two, unit_two, rstd_two, normed_two
    )
    weight_last(2)
    weight_last(3)
    for copy in og_copies:
        copy.wait_recv()
    own_og.wait()
    for kind in (2, 3):
        weight_own(kind)
        weight_ready(kind)

    def core_send(view_src, view_dst):
        return send(view_src, view_dst, core)

    def add_core(u, jy, row, rows):
        def step(i):
            r = span(row + i * 64, 64)
            part[u, jy, hc, r, :] = (
                part[u, jy, hc, r, :].astype(F32) + buf_core[u, jy, r, :].astype(F32)
            ).astype(BF16)

        loop(rows // 64, step)

    owner = None if pairs == OWNERS else pair < OWNERS

    class Chunk:
        def __init__(self, n):
            self.u, self.row, self.rows, self.lane, self.lanes, self.y_first = CHUNKS[n]
            self.half = self.rows // 2
            self.piece = self.half // OWNERS
            self.buf, self.ring_buf, self.own = chunk_refs[3 * n : 3 * n + 3]
            self.cols = pl.ds(self.lane, self.lanes)
            self.devices = (ypeer, xpeer) if self.y_first else (xpeer, ypeer)
            self.ring_base = self.spread_base = None

        def rows_of(self, half, at=0, size=None):
            return span(self.row + half * self.half + at, size or self.half, 16)

        def at(self, jy, half):
            return part.at[self.u, jy, hc, self.rows_of(half), self.cols]

        def a(self):
            self.first = send(self.at(1 - hy, 1 - par), self.buf.at[0], self.devices[0])

        def b(self):
            source = (1 - hy, par) if self.y_first else (hy, 1 - par)
            self.other = send(self.at(*source), self.buf.at[1], self.devices[0])

        def mid(self):
            self.first.wait_recv()
            jy, half = (hy, 1 - par) if self.y_first else (1 - hy, par)

            def step(i):
                r = self.rows_of(half, i * self.piece, self.piece)
                got = self.buf[0, span(i * self.piece, self.piece), :].astype(F32)
                part[self.u, jy, hc, r, self.cols] = (
                    part[self.u, jy, hc, r, self.cols].astype(F32) + got
                ).astype(BF16)

            loop(OWNERS, step)
            self.second = send(self.at(jy, half), self.buf.at[2], self.devices[1])

        def ring_copy(self, d):
            to, device = ring(d)
            rows = self.rows_of(par, lax.rem(to, OWNERS) * self.piece, self.piece)
            copy = remote(
                part.at[self.u, hy, hc, rows, self.cols],
                self.ring_buf.at[d - 1],
                device,
                self.ring_base + d - 1,
            )
            return copy, None if pairs == OWNERS else to < OWNERS

        def ring(self):
            self.other.wait_recv()
            self.second.wait_recv()

            def step(i):
                r = self.rows_of(par, i * self.piece, self.piece)
                b = span(i * self.piece, self.piece)
                got = self.buf[1, b, :].astype(F32) + self.buf[2, b, :].astype(F32)
                part[self.u, hy, hc, r, self.cols] = (
                    part[self.u, hy, hc, r, self.cols].astype(F32) + got
                ).astype(BF16)

            loop(OWNERS, step)
            self.ring_base = take(pairs - 1)

            def go(d):
                copy, cond = self.ring_copy(d)
                guarded(cond, copy.start)

            each_ring(go)

        def final(self, index):
            rows = self.rows_of(par, lax.rem(index, OWNERS) * self.piece, self.piece)
            return fin.at[self.u, rows, self.cols]

        def spread_copy(self, d):
            return remote(
                self.own, self.final(pair), ring(d)[1], self.spread_base + d - 1
            )

        def spread(self):
            self.spread_base = take(pairs - 1)
            sem = local_sem.at[next(local_ids)]
            self.kept = pltpu.make_async_copy(self.own, self.final(pair), sem)

            def total():
                each_ring(lambda d: self.ring_copy(d)[0].wait_recv())
                rows = self.rows_of(par, lax.rem(pair, OWNERS) * self.piece, self.piece)
                self.own[...] = part[self.u, hy, hc, rows, self.cols]

                def more(d):
                    self.own[...] = (
                        self.own[...].astype(F32) + self.ring_buf[d - 1].astype(F32)
                    ).astype(BF16)

                if pairs == OWNERS:
                    value = part[self.u, hy, hc, rows, self.cols].astype(F32)
                    for d in range(1, pairs):
                        value = value + self.ring_buf[d - 1].astype(F32)
                    self.own[...] = value.astype(BF16)
                else:
                    each_ring(more)
                each_ring(lambda d: self.spread_copy(d).start())
                self.kept.start()

            guarded(owner, total)

        def back(self):
            def arrived(d):
                giver = lax.rem(pair - d + pairs, pairs)
                cond = None if pairs == OWNERS else giver < OWNERS
                guarded(cond, self.spread_copy(d).wait_recv)

            each_ring(arrived)
            guarded(owner, self.kept.wait)
            rows = fin.at[self.u, self.rows_of(par), self.cols]
            self.last = send(rows, rows, xpeer)

        def end(self):
            self.last.wait_recv()

        def sent(self):
            def one(d):
                copy, cond = self.ring_copy(d)
                guarded(cond, copy.wait_send)

            each_ring(one)
            guarded(owner, lambda: each_ring(lambda d: self.spread_copy(d).wait_send()))

    d0, d1, u0, u1, o0, a0, a1 = chunks = [Chunk(n) for n in range(len(CHUNKS))]

    def zero_rows(r):
        ffn[r, :] = jnp.zeros((64, 512), F32)
        norm_grad[r, :] = jnp.zeros((64, 512), F32)

    rows_loop(512, 64, zero_rows)

    def feed(jy):
        base = take()
        copy = remote(part.at[0:2, jy, 1 - hc], buf_core.at[0:2, jy], core, base)

        def one(i):
            jc = lax.rem(1 - hc + i, 2)
            j = 2 * jy + jc
            work[...] = mm(normed_two[...], w_u[j])
            work_two[...] = mm(ogs[...], w_d[j], "NT")

            def step(r):
                v = work[r, :]
                sigma = 1.0 / (1.0 + jnp.exp(-v))
                hid[r, :] = (v * sigma).astype(BF16)
                hid_grad[r, :] = (work_two[r, :] * (sigma * (1.0 + v * (1.0 - sigma)))).astype(
                    BF16
                )

            rows_loop(512, 64, step)
            part[0, jy, jc] = mm(hid[...], ogs[...], "TN").astype(BF16)
            part[1, jy, jc] = mm(normed_two[...], hid_grad[...], "TN").astype(BF16)

            @pl.when(i == 0)
            def _():
                copy.start()

            ffn[...] += mm(hid[...], w_d[j])
            norm_grad[...] += mm(hid_grad[...], w_u[j], "NT")

        loop(2, one)
        sends.append(copy)
        copy.wait_recv()
        add_core(0, jy, 0, 512)
        add_core(1, jy, 0, 512)

    feed(1 - hy)
    d0.a()
    u0.a()
    d1.a()
    u1.a()
    feed(hy)
    u0.b()
    u1.b()
    d0.b()
    d1.b()

    gain_part[0] = jnp.zeros((8, 512), F32)
    row_512 = lax.broadcasted_iota(jnp.int32, (8, 512), 0)

    def norm_back(grad_ref, gain, unit_ref, rstd_ref, base, sink, row):
        def step(r):
            grad = grad_ref[r, :]
            unit = unit_ref[r, :]
            scaled = grad * gain[...]
            mean_one = jnp.mean(scaled, axis=-1, keepdims=True)
            mean_two = jnp.mean(scaled * unit, axis=-1, keepdims=True)
            rstd = rstd_ref[r, :]
            rstd = jnp.concatenate([rstd] * 4, axis=1)
            sink(r, base(r) + rstd * (scaled - mean_one - unit * mean_two))
            total = jnp.sum(grad * unit, axis=0, keepdims=True)
            gain_part[0] = gain_part[0] + jnp.where(row_512 == row, total, 0.0)

        rows_loop(512, 64, step)

    def sink_middle(r, grad):
        middle_grad[r, :] = grad
        middle_low[r, :] = grad.astype(BF16)
        lo_s[r, :] = (middle[r, :] + ffn[r, :]).astype(BF16)

    norm_back(
        norm_grad, gain_two, unit_two, rstd_two, lambda r: ogs[r, :].astype(F32), sink_middle, 1
    )

    out_rows = pl.ds(384, 128)
    work_two[...] = mm(attn[...], middle_low[...], "TN")
    for j in range(4):
        part[2, j // 2, j % 2, out_rows, :] = work_two[j * 128 : (j + 1) * 128, :].astype(BF16)
    core_o = core_send(part.at[2, :, 1 - hc, out_rows], buf_core.at[2, :, out_rows])
    work[...] = mm(middle_low[...], w_o[...], "NT")

    head_ones = jnp.where(spread, 1.0, 0.0).astype(BF16)
    head_ones = jnp.concatenate([head_ones, head_ones], axis=0)
    first_lane = lax.rem(lane, 64) == 0
    second_lane = lax.rem(lane, 64) == 1

    def split(wide):
        high = wide.astype(BF16)
        return high, (wide - high.astype(F32)).astype(BF16)

    grad_z[...] = jnp.zeros_like(grad_z)

    def outer(i):
        b, pr, rows, cols = place(i)
        grad, inverse = work[rows, cols], den_inv[rows, cols]
        gnum = (grad * inverse).astype(BF16)
        high, low = split(grad * attn_wide[rows, cols])
        gden = -mm(jnp.concatenate([high, low], axis=1), head_ones) * inverse
        dhigh = gden.astype(BF16).astype(F32)
        num_grad[rows, cols] = gnum
        den_grad[rows, cols] = jnp.where(
            first_lane, dhigh, jnp.where(second_lane, gden - dhigh, 0.0)
        ).astype(BF16)
        queries = feat[0, rows, cols].astype(F32) * carry_on[b]
        grad_s[b, packed_rows(pr), :] = pack(mm(queries.astype(BF16), gnum, "TN"))
        grad_z[b, pl.ds(pr, 1), :] = jnp.sum(queries * gden, axis=0, keepdims=True)

    loop(8, outer)
    msg_gs[...] = (grad_s[0] + keep_first * grad_s[1]).astype(BF16)
    msg_gz[...] = jnp.where(row8 == 4, keep_first * keep_mid, grad_z[0] + keep_first * grad_z[1])
    backward = {}
    for d in (1, 2):
        pieces = [(msg_gs, buf_gs.at[d - 1]), (msg_gz, buf_gz.at[d - 1])]
        backward[d] = shift(-d, pieces, take(2))

        @pl.when(pair >= d)
        def _():
            for copy in backward[d]:
                copy.start()

    d0.mid()
    u0.mid()
    core_o.wait_recv()
    add_core(2, 0, 384, 128)
    add_core(2, 1, 384, 128)
    o0.a()
    o0.b()

    marks = jnp.where(first_lane | second_lane, 1.0, 0.0).astype(BF16)
    marks = jnp.broadcast_to(marks, (256, 128))

    def inner(i):
        b, pr, rows, cols = place(i)
        q, k, v = feat[0, rows, cols], feat[1, rows, cols], val[rows, cols]
        gnum, gden = num_grad[rows, cols], den_grad[rows, cols]
        gnum_two = two(gnum)
        grads = jnp.concatenate([gnum_two, two(gden)], axis=1)
        values = jnp.concatenate([v, marks], axis=1)
        m = mask[b]
        gsc = mm(grads, values, "NT")
        gsc = jnp.concatenate([gsc[:256] * m, gsc[256:] * m], axis=0).astype(BF16)
        qgrad = pick(mm(gsc, k)) + carry_on[b] * mm(
            jnp.concatenate([gnum, gden], axis=1), state[i], "NT"
        )
        low_grads[0, rows, cols] = (qgrad * jnp.minimum(q.astype(F32), 1.0)).astype(BF16)
        key_acc[rows, cols] = mm(gsc, two(q), "TN")
        val_acc[rows, cols] = mm(scores_low[i], gnum_two, "TN")

    loop(8, inner)

    d1.mid()
    u1.mid()
    o0.mid()
    for d in (1, 2):

        @pl.when(pair + d < pairs)
        def _():
            for copy in backward[d]:
                copy.wait_recv()

    pass_on = buf_gz[0, pl.ds(4, 1), :]
    buf_gz[0] = buf_gz[0] + pass_on * buf_gz[1]

    def leave(i):
        b, pr, rows, cols = place(i)
        leaving = buf_gs[0, packed_rows(pr), :].astype(F32) + pass_on * buf_gs[
            1, packed_rows(pr), :
        ].astype(F32)
        z_leaving = buf_gz[0, pl.ds(pr, 1), :]
        first_block = (1 - b).astype(F32)
        scale = first_block * keep_mid + (1.0 - first_block)
        leaving = scale * leaving + first_block * grad_s[1, packed_rows(pr), :]
        z_leaving = scale * z_leaving + first_block * grad_z[1, pl.ds(pr, 1), :]
        square = two(leaving).astype(BF16)
        k, v = feat[1, rows, cols], val[rows, cols]
        tail = seg_col[b] == seg_col[b, pl.ds(255, 1), :]
        kgrad = key_acc[rows, cols] + jnp.where(tail, mm(v, square, "NT") + z_leaving, 0.0)
        low_grads[1, rows, cols] = (kgrad * jnp.minimum(k.astype(F32), 1.0)).astype(BF16)
        vgrad = val_acc[rows, cols] + jnp.where(tail, mm(k, square), 0.0)
        low_grads[2, rows, cols] = vgrad.astype(BF16)

    loop(8, leave)

    def qkv_weight(i):
        work[...] = mm(low_grads[i], normed[...], "TN")
        for j in range(4):
            part[2, j // 2, j % 2, at128(i), :] = work[j * 128 : (j + 1) * 128, :].astype(BF16)

    loop(3, qkv_weight)
    qkv_rows = pl.ds(0, 384)
    core_a = [
        core_send(part.at[2, jy, 1 - hc, qkv_rows], buf_core.at[2, jy, qkv_rows])
        for jy in (1 - hy, hy)
    ]
    norm_grad[...] = mm(low_grads[0], w_qkv[0], "NT")
    core_a[0].wait_recv()
    add_core(2, 1 - hy, 0, 384)
    a0.a()
    a1.a()
    core_a[1].wait_recv()
    add_core(2, hy, 0, 384)
    a1.b()
    a0.b()
    d0.ring()
    u0.ring()
    norm_grad[...] += mm(low_grads[1], w_qkv[1], "NT")
    norm_grad[...] += mm(low_grads[2], w_qkv[2], "NT")
    lo_copies, lo_own = scatter_out(lo_s, lo_out)

    def sink_input(r, grad):
        ig_s[r, :] = grad.astype(BF16)

    norm_back(norm_grad, gain_one, unit_one, rstd_one, lambda r: middle_grad[r, :], sink_input, 0)

    def gain_stage(n, device):
        copy = send(gain_part.at[n], gain_buf.at[n], device)
        copy.wait_recv()
        gain_part[n + 1] = gain_part[n] + gain_buf[n]

    a0.mid()
    a1.mid()
    d1.ring()
    u1.ring()
    o0.ring()
    d0.spread()
    u0.spread()
    ig_copies, ig_own = scatter_out(ig_s, ig_out)
    a0.ring()
    a1.ring()
    gain_stage(0, core)
    d1.spread()
    u1.spread()
    o0.spread()
    d0.back()
    u0.back()
    gain_stage(1, ypeer)
    a0.spread()
    a1.spread()
    gain_stage(2, xpeer)
    gain_base = take(pairs - 1)

    def gain_copy(d):
        return remote(gain_part.at[3], gain_buf.at[2 + d], ring(d)[1], gain_base + d - 1)

    each_ring(lambda d: gain_copy(d).start())
    d1.back()
    u1.back()
    o0.back()
    a0.back()
    a1.back()
    each_ring(lambda d: gain_copy(d).wait_recv())
    gain_part[4] = gain_part[3]

    def add_gain(d):
        gain_part[4] = gain_part[4] + gain_buf[2 + d]

    each_ring(add_gain)
    gains[...] = gain_part[4, :, hcol]

    for chunk in chunks:
        chunk.end()
    for copy in lo_copies + ig_copies:
        copy.wait_recv()
    lo_own.wait()
    ig_own.wait()
    for copy in sends:
        copy.wait_send()
    for chunk in chunks:
        chunk.sent()
    each_ring(lambda d: gain_copy(d).wait_send())
    for d in (1, 2):

        @pl.when(pair + d < pairs)
        def _():
            for order in range(2):
                for copy in forward[order, d]:
                    copy.wait_send()

        @pl.when(pair >= d)
        def _():
            for copy in backward[d]:
                copy.wait_send()


def widen_kernel(lo, ig, fin_d, fin_u, fin_a, gains, lo_o, ig_o, q_o, k_o, v_o, o_o, u_o, d_o, g_o, f_o):
    step = pl.program_id(0)
    lo_o[...] = lo[...]
    ig_o[...] = ig[...].astype(F32)
    d_o[...] = fin_d[0].astype(F32)
    u_o[...] = fin_u[0].astype(F32)
    for i, out in enumerate((q_o, k_o, v_o)):

        @pl.when(step == i)
        def _():
            out[...] = fin_a[0].astype(F32).T

    @pl.when(step == 3)
    def _():
        o_o[...] = fin_a[0].astype(F32)

    g_o[...] = gains[0]
    f_o[...] = gains[1]


def body(
    tokens,
    norm_gain,
    query_weight,
    key_weight,
    value_weight,
    attention_output_weight,
    feedforward_norm_gain,
    up_weight,
    down_weight,
    segment_ids,
    out_grad,
):
    batch, length, share = tokens.shape
    width, head_cols = query_weight.shape
    units = up_weight.shape[1]
    pairs = lax.axis_size("seq") // 2
    assert lax.axis_size("head") == 4 and batch == 8 and length == BLOCK
    assert (width, share, head_cols, units) == (512, 128, 128, 512)
    assert pairs >= OWNERS and pairs % 2 == 0
    others = pairs - 1
    anywhere = pl.BlockSpec(memory_space=pl.ANY)
    vmem = pl.BlockSpec(memory_space=pltpu.VMEM)
    copies = 7 * 4 + 1 + 10 * KINDS + 8 + 4 + 5 + len(CHUNKS) * (4 + 2 * others) + 3 + others
    square = (512, 512)
    buffers = dict(
        xin=(square, BF16),
        ogs=(square, BF16),
        w_qkv=((3, 512, 512), BF16),
        w_o=(square, BF16),
        w_u=((4, 512, 512), BF16),
        w_d=((4, 512, 512), BF16),
        seg_other=((8, 256), jnp.int32),
        unit_one=(square, F32),
        unit_two=(square, F32),
        rstd_one=((512, 128), F32),
        rstd_two=((512, 128), F32),
        normed=(square, BF16),
        normed_two=(square, BF16),
        feat=((2, 512, 512), BF16),
        val=(square, BF16),
        mask=((2, 256, 256), F32),
        seg_col=((2, 256, 128), F32),
        carry_on=((2, 256, 128), F32),
        own_s=((2, 256, 128), F32),
        own_z=((2, 8, 128), F32),
        msg_s=((256, 128), BF16),
        msg_z=((2, 8, 128), F32),
        buf_s=((2, 256, 128), BF16),
        buf_z=((2, 2, 8, 128), F32),
        state=((8, 128, 256), BF16),
        scores_low=((8, 512, 256), BF16),
        attn=(square, BF16),
        attn_wide=(square, F32),
        den_inv=(square, F32),
        middle=(square, F32),
        work=(square, F32),
        work_two=(square, F32),
        hid=(square, BF16),
        hid_grad=(square, BF16),
        ffn=(square, F32),
        norm_grad=(square, F32),
        middle_grad=(square, F32),
        middle_low=(square, BF16),
        num_grad=(square, BF16),
        den_grad=(square, BF16),
        grad_s=((2, 256, 128), F32),
        grad_z=((2, 8, 128), F32),
        msg_gs=((256, 128), BF16),
        msg_gz=((8, 128), F32),
        buf_gs=((2, 256, 128), BF16),
        buf_gz=((2, 8, 128), F32),
        key_acc=(square, F32),
        val_acc=(square, F32),
        low_grads=((3, 512, 512), BF16),
        lo_s=(square, BF16),
        ig_s=(square, BF16),
        part=((3, 2, 2, 512, 512), BF16),
        buf_core=((3, 2, 512, 512), BF16),
        gain_part=((5, 8, 512), F32),
        gain_buf=((3 + others, 8, 512), F32),
    )
    shapes = list(buffers.values())
    for _, _, rows, _, lanes, _ in CHUNKS:
        piece = rows // 2 // OWNERS
        shapes.append(((3, rows // 2, lanes), BF16))
        shapes.append(((others, piece, lanes), BF16))
        shapes.append(((piece, lanes), BF16))
    scratch = [pltpu.VMEM(*spec) for spec in shapes]
    scratch += [
        pltpu.SemaphoreType.DMA((8 + 2 + len(CHUNKS),)),
        pltpu.SemaphoreType.DMA((copies,)),
        pltpu.SemaphoreType.DMA((copies,)),
    ]
    lo, ig, fin, gains = pl.pallas_call(
        functools.partial(layer_kernel, pairs, list(buffers)),
        out_shape=(
            jax.ShapeDtypeStruct((batch, length, share), BF16),
            jax.ShapeDtypeStruct((batch, length, share), BF16),
            jax.ShapeDtypeStruct((3, 512, 512), BF16),
            jax.ShapeDtypeStruct((8, 128), F32),
        ),
        in_specs=[anywhere] * 8 + [vmem] * 3,
        out_specs=(anywhere, anywhere, anywhere, vmem),
        scratch_shapes=scratch,
        compiler_params=pltpu.CompilerParams(
            collective_id=0, has_side_effects=True, vmem_limit_bytes=58 * MIB
        ),
        cost_estimate=pl.CostEstimate(
            flops=11 * 10**9, bytes_accessed=8 * MIB, transcendentals=4 * 10**6
        ),
        name="layer",
    )(
        tokens,
        out_grad,
        query_weight,
        key_weight,
        value_weight,
        attention_output_weight,
        up_weight,
        down_weight,
        segment_ids,
        norm_gain[None],
        feedforward_norm_gain[None],
    )

    def whole(shape):
        return pl.BlockSpec(shape, lambda g: (0,) * len(shape))

    def rows_block(u):
        return pl.BlockSpec((1, 128, 512), lambda g: (u, g, 0))

    tok_block = pl.BlockSpec((batch // 4, length, share), lambda g: (g, 0, 0))
    wide_block = pl.BlockSpec((128, 512), lambda g: (g, 0))
    lo, ig, q_w, k_w, v_w, o_w, u_w, d_w, g_one, g_two = pl.pallas_call(
        widen_kernel,
        grid=(4,),
        out_shape=(
            jax.ShapeDtypeStruct((batch, length, share), BF16),
            jax.ShapeDtypeStruct((batch, length, share), F32),
            jax.ShapeDtypeStruct((512, 128), F32),
            jax.ShapeDtypeStruct((512, 128), F32),
            jax.ShapeDtypeStruct((512, 128), F32),
            jax.ShapeDtypeStruct((128, 512), F32),
            jax.ShapeDtypeStruct((512, 512), F32),
            jax.ShapeDtypeStruct((512, 512), F32),
            jax.ShapeDtypeStruct((128,), F32),
            jax.ShapeDtypeStruct((128,), F32),
        ),
        in_specs=[
            tok_block,
            tok_block,
            rows_block(0),
            rows_block(1),
            rows_block(2),
            whole((8, 128)),
        ],
        out_specs=(
            tok_block,
            tok_block,
            whole((512, 128)),
            whole((512, 128)),
            whole((512, 128)),
            whole((128, 512)),
            wide_block,
            wide_block,
            whole((128,)),
            whole((128,)),
        ),
        compiler_params=pltpu.CompilerParams(vmem_limit_bytes=58 * MIB),
        name="widen",
    )(lo, ig, fin, fin, fin, gains)
    return (lo, ig, g_one, q_w, k_w, v_w, o_w, g_two, u_w, d_w)


def solution(mesh):
    in_specs = (
        P(None, "seq", "head"),
        P(),
        P(None, "head"),
        P(None, "head"),
        P(None, "head"),
        P("head", None),
        P(),
        P(None, "head"),
        P("head", None),
        P(None, "seq"),
        P(None, "seq", "head"),
    )
    out_specs = (
        P(None, "seq", "head"),
        P(None, "seq", "head"),
        P("head"),
        P(None, "head"),
        P(None, "head"),
        P(None, "head"),
        P("head", None),
        P("head"),
        P(None, "head"),
        P("head", None),
    )
    return jax.shard_map(body, mesh=mesh, in_specs=in_specs, out_specs=out_specs, check_vma=False)
```

time: 157 us -> 123 us (0.78)
  Pallas kernels: 152 us -> 122 us
  local copies, waits for them, and re-layouts: 4.52 us -> 0 us
    pallas_call x2, Pallas kernels: 152 us -> 122 us  [the longest x1 117 us: body(): pl.pallas_call(functools.partial(layer_kernel, pairs, list(buffers)), out...]
    unnamed x7 -> x0, local copies, waits for them, and re-layouts: 3.25 us -> none
where the time goes in v2:
time: 123 us
  Pallas kernels  122 us (99%)
    pallas_call x1, Pallas kernels, body(): pl.pallas_call(functools.partial(layer_kernel, pairs, list(buffers)), out...  117 us
    pallas_call x1, Pallas kernels, body(): pl.pallas_call(widen_kernel, grid=(4,), out_shape=(jax.ShapeDtypeStruct((...  4.92 us

profile of v2, /device:TPU:0, one launch (start us, length us, event | category | flops | bytes accessed | tf_op | source)
XLA Modules:
  0.0 122.7 jit_solution(12887167318927963747)
XLA Ops:
  0.6 117.1 %layer.1 = (bf16[8,256,128]{2,1,0:T(8,128)(2,1)}, bf16[8,256,128]{2,1,0:T(8,128)(2,1)}, bf16[3,512,512]{2,1,0:T(8,128)(2,1)}, f32[8,128]{1,0:T(8,128)}) custom-call(bf16[8,256,128]{2,1,0:T(8,128)(2,1)} %refs_0_.1, bf16[8,256,128]{2,1,0:T(8,128)(2,1)} %refs_1_.1, bf16[512,128]{1,0:T(8,128)(2,1)} %refs_2_.1, bf16[512,128]{1,0:T(8,128)(2,1)} %refs_3_.1, ...), custom_call_target="tpu_custom_call" | custom-call | flops 11000000512 | bytes 8388608 | tf_op jit(solution)/shard_map/layer/pallas_call | solution.py:1052
  117.7 4.9 %widen.1 = (bf16[8,256,128]{2,1,0:T(8,128)(2,1)}, f32[8,256,128]{2,1,0:T(8,128)}, f32[512,128]{1,0:T(8,128)}, f32[512,128]{1,0:T(8,128)}, f32[512,128]{1,0:T(8,1...) custom-call(bf16[8,256,128]{2,1,0:T(8,128)(2,1)} %get-tuple-element.24.lo, ...), custom_call_target="tpu_custom_call" | custom-call | tf_op jit(solution)/shard_map/widen/pallas_call | solution.py:1092

commit v3 on v2

--- a/solution.py
+++ b/solution.py
@@ -21,7 +21,7 @@
     (0, 0, 512, 0, 256, True),
     (0, 0, 512, 256, 256, True),
     (1, 0, 512, 0, 256, False),
-    (1, 0, 512, 256, 256, False),
+    (1, 0, 512, 256, 256, True),
     (2, 384, 128, 0, 512, True),
     (2, 0, 384, 0, 256, True),
     (2, 0, 384, 256, 256, False),
@@ -90,6 +90,7 @@
     key_acc, val_acc, low_grads, lo_s, ig_s = (
         r_.key_acc, r_.val_acc, r_.low_grads, r_.lo_s, r_.ig_s,
     )
+    gain_sum = r_.gain_sum
     part, buf_core, gain_part, gain_buf, seg_other = (
         r_.part, r_.buf_core, r_.gain_part, r_.gain_buf, r_.seg_other,
     )
@@ -188,9 +189,9 @@
     )
     pl.semaphore_wait(barrier, len(COMBOS) + pairs - 1)
 
-    def scatter_in(src, dst):
+    def scatter_in(src, dst, combos=COMBOS):
         copies = []
-        for d in COMBOS:
+        for d in combos:
             par_to, y_to, c_to = peer(*d)
             copies.append(
                 send(
@@ -201,9 +202,9 @@
             )
         return copies
 
-    def scatter_out(src, dst):
+    def scatter_out(src, dst, combos):
         copies = []
-        for d in COMBOS:
+        for d in combos:
             par_to, y_to, c_to = peer(*d)
             copies.append(
                 send(
@@ -212,13 +213,11 @@
                     address(par_to, y_to, c_to),
                 )
             )
-        return copies, local(src.at[half256, hcol], dst.at[member])
+        return copies
 
     across = 2 * (1 - hy) + hc
     quarter = par + 2 * zb
     quarter_x = 1 - par + 2 * zb
-    quarter_z = par + 2 * (1 - zb)
-    quarter_far = 1 - par + 2 * (1 - zb)
 
     def view(kind, shard, eighth=None, eighths=2):
         rows = 32 if kind == 1 else 128
@@ -252,20 +251,16 @@
         wt[kind, "y"].wait_recv()
         wt[kind, "x"] = pass_on_weight(kind, 2 * quarter, 2, xpeer)
         wt[kind, "z"] = pass_on_weight(kind, 2 * quarter, 2, zpeer)
-        wt[kind, "c"].append(pass_on_weight(kind, 2 * quarter, 2, core))
 
     def weight_far(kind):
         wt[kind, "x"].wait_recv()
-        wt[kind, "z2"] = pass_on_weight(kind, 2 * quarter_x, 1, zpeer)
-        wt[kind, "c"].append(pass_on_weight(kind, 2 * quarter_x, 2, core))
+        wt[kind, "far"] = pass_on_weight(kind, 2 * quarter_x, 2, zpeer)
+        wt[kind, "c"].append(pass_on_weight(kind, 4 * zb, 4, core))
+
+    def weight_last(kind):
         wt[kind, "z"].wait_recv()
-        wt[kind, "x2"] = pass_on_weight(kind, 2 * quarter_z + 1, 1, xpeer)
-        wt[kind, "c"].append(pass_on_weight(kind, 2 * quarter_z, 2, core))
-
-    def weight_last(kind):
-        wt[kind, "z2"].wait_recv()
-        wt[kind, "x2"].wait_recv()
-        wt[kind, "c"].append(pass_on_weight(kind, 2 * quarter_far, 2, core))
+        wt[kind, "far"].wait_recv()
+        wt[kind, "c"].append(pass_on_weight(kind, 4 * (1 - zb), 4, core))
 
     def weight_own(kind):
         wt[kind, "c"][0].wait_recv()
@@ -283,13 +278,15 @@
     for kind in (1, 2, 3):
         for copy in own_w[kind]:
             copy.wait()
+        weight_y(kind)
+    for kind in (1, 2, 3):
         weight_core(kind)
     weight_near(0)
+    og_copies = scatter_in(og_in, ogs)
     for copy in tokens_in:
         copy.wait_recv()
     own_tok.wait()
-    for kind in (1, 2, 3):
-        weight_y(kind)
+    weight_far(0)
 
     def norm_rows(source, gain, unit_ref, rstd_ref, out_ref):
         def step(r):
@@ -319,7 +316,6 @@
         down = along.T
         mask[b] = jnp.where((along == down) & (second <= first), 1.0, 0.0)
         seg_col[b] = down[:, :128]
-    weight_far(0)
     weight_own(0)
 
     lane = lax.broadcasted_iota(jnp.int32, (1, 128), 1)
@@ -410,15 +406,14 @@
     own_z[...] = jnp.zeros_like(own_z)
     project(hy)
     send_state(0, hy)
+    weight_near(1)
     weight_last(0)
-    og_copies = scatter_in(og_in, ogs)
-    weight_near(1)
+    weight_near(2)
     weight_ready(0)
     project(1 - hy)
     send_state(1, 1 - hy)
-    weight_near(2)
+    weight_far(1)
     weight_near(3)
-    weight_far(1)
 
     ones = jnp.ones((256, 128), BF16)
     ready = {}
@@ -473,18 +468,19 @@
         attn_wide[rows, cols] = result
         attn[rows, cols] = result.astype(BF16)
 
-    for order, side in ((0, hy), (1, 1 - hy)):
-        receive_state(order)
-        enter(order, side)
-        loop(4, lambda i: attend(i, side))
-        if order == 0:
-            weight_last(1)
-            weight_far(2)
+    receive_state(0)
+    enter(0, hy)
+    loop(4, lambda i: attend(i, hy))
+    weight_far(2)
+    receive_state(1)
+    enter(1, 1 - hy)
+    weight_last(1)
+    loop(4, lambda i: attend(i, 1 - hy))
     keep_first = ready["keep_first"]
-    weight_far(3)
     weight_own(1)
     weight_ready(1)
 
+    weight_far(3)
     work[...] = mm(attn[...], w_o[...])
 
     def mid_step(r):
@@ -494,14 +490,11 @@
     norm_rows(
         lambda r: middle[r, :].astype(BF16).astype(F32), gain_two, unit_two, rstd_two, normed_two
     )
-    weight_last(2)
-    weight_last(3)
     for copy in og_copies:
         copy.wait_recv()
     own_og.wait()
-    for kind in (2, 3):
-        weight_own(kind)
-        weight_ready(kind)
+    weight_own(2)
+    weight_own(3)
 
     def core_send(view_src, view_dst):
         return send(view_src, view_dst, core)
@@ -652,51 +645,57 @@
 
     rows_loop(512, 64, zero_rows)
 
-    def feed(jy):
-        base = take()
-        copy = remote(part.at[0:2, jy, 1 - hc], buf_core.at[0:2, jy], core, base)
-
-        def one(i):
-            jc = lax.rem(1 - hc + i, 2)
-            j = 2 * jy + jc
-            work[...] = mm(normed_two[...], w_u[j])
-            work_two[...] = mm(ogs[...], w_d[j], "NT")
-
-            def step(r):
-                v = work[r, :]
-                sigma = 1.0 / (1.0 + jnp.exp(-v))
-                hid[r, :] = (v * sigma).astype(BF16)
-                hid_grad[r, :] = (work_two[r, :] * (sigma * (1.0 + v * (1.0 - sigma)))).astype(
-                    BF16
-                )
-
-            rows_loop(512, 64, step)
-            part[0, jy, jc] = mm(hid[...], ogs[...], "TN").astype(BF16)
-            part[1, jy, jc] = mm(normed_two[...], hid_grad[...], "TN").astype(BF16)
-
-            @pl.when(i == 0)
-            def _():
-                copy.start()
-
-            ffn[...] += mm(hid[...], w_d[j])
-            norm_grad[...] += mm(hid_grad[...], w_u[j], "NT")
-
-        loop(2, one)
-        sends.append(copy)
+    def feed(jc, jy):
+        j = 2 * jy + jc
+        work[...] = mm(normed_two[...], w_u[j])
+        work_two[...] = mm(ogs[...], w_d[j], "NT")
+
+        def step(r):
+            v = work[r, :]
+            sigma = 1.0 / (1.0 + jnp.exp(-v))
+            hid[r, :] = (v * sigma).astype(BF16)
+            hid_grad[r, :] = (work_two[r, :] * (sigma * (1.0 + v * (1.0 - sigma)))).astype(BF16)
+
+        rows_loop(512, 64, step)
+        part[0, jy, jc] = mm(hid[...], ogs[...], "TN").astype(BF16)
+        part[1, jy, jc] = mm(normed_two[...], hid_grad[...], "TN").astype(BF16)
+
+    def feed_on(jc, jy):
+        j = 2 * jy + jc
+        ffn[...] += mm(hid[...], w_d[j])
+        norm_grad[...] += mm(hid_grad[...], w_u[j], "NT")
+
+    def core_feed(jy):
+        return core_send(part.at[0:2, jy, 1 - hc], buf_core.at[0:2, jy])
+
+    def core_fed(copy, jy):
         copy.wait_recv()
         add_core(0, jy, 0, 512)
         add_core(1, jy, 0, 512)
 
-    feed(1 - hy)
-    d0.a()
+    feed(1 - hc, hy)
+    core_f = core_feed(hy)
+    feed_on(1 - hc, hy)
+    weight_last(2)
+    feed(hc, hy)
+    core_fed(core_f, hy)
+    u0.b()
+    weight_last(3)
+    feed_on(hc, hy)
+    weight_ready(2)
+    weight_ready(3)
+    feed(1 - hc, 1 - hy)
+    core_f = core_feed(1 - hy)
+    feed_on(1 - hc, 1 - hy)
+    feed(hc, 1 - hy)
+    core_fed(core_f, 1 - hy)
+    for chunk in (d0, d1):
+        chunk.a()
+        chunk.b()
     u0.a()
-    d1.a()
     u1.a()
-    feed(hy)
-    u0.b()
     u1.b()
-    d0.b()
-    d1.b()
+    feed_on(hc, 1 - hy)
 
     gain_part[0] = jnp.zeros((8, 512), F32)
     row_512 = lax.broadcasted_iota(jnp.int32, (8, 512), 0)
@@ -725,6 +724,8 @@
         norm_grad, gain_two, unit_two, rstd_two, lambda r: ogs[r, :].astype(F32), sink_middle, 1
     )
 
+    lo_copies = scatter_out(lo_s, lo_out, COMBOS[4:])
+    lo_own = local(lo_s.at[half256, hcol], lo_out.at[member])
     out_rows = pl.ds(384, 128)
     work_two[...] = mm(attn[...], middle_low[...], "TN")
     for j in range(4):
@@ -770,14 +771,6 @@
         def _():
             for copy in backward[d]:
                 copy.start()
-
-    d0.mid()
-    u0.mid()
-    core_o.wait_recv()
-    add_core(2, 0, 384, 128)
-    add_core(2, 1, 384, 128)
-    o0.a()
-    o0.b()
 
     marks = jnp.where(first_lane | second_lane, 1.0, 0.0).astype(BF16)
     marks = jnp.broadcast_to(marks, (256, 128))
@@ -799,11 +792,17 @@
         key_acc[rows, cols] = mm(gsc, two(q), "TN")
         val_acc[rows, cols] = mm(scores_low[i], gnum_two, "TN")
 
-    loop(8, inner)
+    loop(4, inner)
+    d0.mid()
+    u0.mid()
+    core_o.wait_recv()
+    add_core(2, 0, 384, 128)
+    add_core(2, 1, 384, 128)
+    loop(4, lambda i: inner(4 + i))
 
     d1.mid()
-    u1.mid()
-    o0.mid()
+    o0.a()
+    o0.b()
     for d in (1, 2):
 
         @pl.when(pair + d < pairs)
@@ -834,6 +833,7 @@
 
     loop(8, leave)
 
+    d0.ring()
     def qkv_weight(i):
         work[...] = mm(low_grads[i], normed[...], "TN")
         for j in range(4):
@@ -852,63 +852,83 @@
     a1.a()
     core_a[1].wait_recv()
     add_core(2, hy, 0, 384)
+    a0.b()
     a1.b()
-    a0.b()
-    d0.ring()
-    u0.ring()
     norm_grad[...] += mm(low_grads[1], w_qkv[1], "NT")
     norm_grad[...] += mm(low_grads[2], w_qkv[2], "NT")
-    lo_copies, lo_own = scatter_out(lo_s, lo_out)
+    u1.mid()
 
     def sink_input(r, grad):
         ig_s[r, :] = grad.astype(BF16)
 
     norm_back(norm_grad, gain_one, unit_one, rstd_one, lambda r: middle_grad[r, :], sink_input, 0)
 
-    def gain_stage(n, device):
-        copy = send(gain_part.at[n], gain_buf.at[n], device)
-        copy.wait_recv()
-        gain_part[n + 1] = gain_part[n] + gain_buf[n]
-
+    def gain_start():
+        copies = []
+        for n, d in enumerate(COMBOS):
+            par_to, y_to, c_to = peer(*d)
+            copies.append(
+                send(
+                    gain_part.at[0, :, at128(2 * y_to + c_to)],
+                    gain_buf.at[n],
+                    address(par_to, y_to, c_to),
+                )
+            )
+        return copies
+
+    gain_base = take(pairs - 1)
+
+    def gain_copy(d):
+        return remote(gain_sum.at[0], gain_buf.at[6 + d], ring(d)[1], gain_base + d - 1)
+
+    def gain_middle(copies):
+        for copy in copies:
+            copy.wait_recv()
+        total = gain_part[0, :, hcol]
+        for n in range(len(COMBOS)):
+            total = total + gain_buf[n]
+        gain_sum[0] = total
+        each_ring(lambda d: gain_copy(d).start())
+
+    def gain_end():
+        each_ring(lambda d: gain_copy(d).wait_recv())
+        gain_sum[1] = gain_sum[0]
+
+        def add_gain(d):
+            gain_sum[1] = gain_sum[1] + gain_buf[6 + d]
+
+        each_ring(add_gain)
+        gains[...] = gain_sum[1]
+
+    gain_copies = gain_start()
+    d1.ring()
+    d0.spread()
+    u0.ring()
+    u1.ring()
+    o0.mid()
+    d1.spread()
+    d0.back()
     a0.mid()
     a1.mid()
-    d1.ring()
-    u1.ring()
     o0.ring()
-    d0.spread()
     u0.spread()
-    ig_copies, ig_own = scatter_out(ig_s, ig_out)
     a0.ring()
     a1.ring()
-    gain_stage(0, core)
-    d1.spread()
+    lo_copies += scatter_out(lo_s, lo_out, COMBOS[:4])
+    ig_copies = scatter_out(ig_s, ig_out, COMBOS)
+    ig_own = local(ig_s.at[half256, hcol], ig_out.at[member])
+    d1.back()
     u1.spread()
+    gain_middle(gain_copies)
     o0.spread()
-    d0.back()
     u0.back()
-    gain_stage(1, ypeer)
     a0.spread()
     a1.spread()
-    gain_stage(2, xpeer)
-    gain_base = take(pairs - 1)
-
-    def gain_copy(d):
-        return remote(gain_part.at[3], gain_buf.at[2 + d], ring(d)[1], gain_base + d - 1)
-
-    each_ring(lambda d: gain_copy(d).start())
-    d1.back()
     u1.back()
     o0.back()
     a0.back()
     a1.back()
-    each_ring(lambda d: gain_copy(d).wait_recv())
-    gain_part[4] = gain_part[3]
-
-    def add_gain(d):
-        gain_part[4] = gain_part[4] + gain_buf[2 + d]
-
-    each_ring(add_gain)
-    gains[...] = gain_part[4, :, hcol]
+    gain_end()
 
     for chunk in chunks:
         chunk.end()
@@ -935,24 +955,59 @@
                 copy.wait_send()
 
 
-def widen_kernel(lo, ig, fin_d, fin_u, fin_a, gains, lo_o, ig_o, q_o, k_o, v_o, o_o, u_o, d_o, g_o, f_o):
-    step = pl.program_id(0)
-    lo_o[...] = lo[...]
-    ig_o[...] = ig[...].astype(F32)
-    d_o[...] = fin_d[0].astype(F32)
-    u_o[...] = fin_u[0].astype(F32)
-    for i, out in enumerate((q_o, k_o, v_o)):
-
-        @pl.when(step == i)
-        def _():
-            out[...] = fin_a[0].astype(F32).T
-
-    @pl.when(step == 3)
-    def _():
-        o_o[...] = fin_a[0].astype(F32)
-
+def widen_kernel(lo, ig, fin, gains, *refs):
+    lo_o, ig_o, q_o, k_o, v_o, o_o, u_o, d_o, g_o, f_o = refs[:10]
+    ig_b, fin_b, lo_b, ig_w, fin_w, qkv_w, sem_in, sem_out = refs[10:]
+    parts = []
+    for u in (0, 1, 2):
+        for half in range(2):
+            rows = pl.ds(half * 256, 256)
+            parts.append((fin.at[u, rows], fin_b.at[u, rows], u, half))
+    for quarter in range(4):
+        rows = pl.ds(quarter * 2, 2)
+        parts.append((ig.at[rows], ig_b.at[rows], 3, quarter))
+    for half in range(2):
+        rows = pl.ds(half * 4, 4)
+        parts.append((lo.at[rows], lo_b.at[rows], 4, half))
+    arriving = [
+        pltpu.make_async_copy(source, into, sem_in.at[n])
+        for n, (source, into, _, _) in enumerate(parts)
+    ]
+    for copy in arriving:
+        copy.start()
     g_o[...] = gains[0]
     f_o[...] = gains[1]
+    leaving = []
+
+    def leave(source, out):
+        copy = pltpu.make_async_copy(source, out, sem_out.at[len(leaving)])
+        copy.start()
+        leaving.append(copy)
+
+    for copy, (_, _, u, n) in zip(arriving, parts, strict=True):
+        copy.wait()
+        if u == 4:
+            rows = pl.ds(n * 4, 4)
+            leave(lo_b.at[rows], lo_o.at[rows])
+        elif u == 3:
+            rows = pl.ds(n * 2, 2)
+            ig_w[rows] = ig_b[rows].astype(F32)
+            leave(ig_w.at[rows], ig_o.at[rows])
+        elif u < 2:
+            rows = pl.ds(n * 256, 256)
+            fin_w[u, rows] = fin_b[u, rows].astype(F32)
+            leave(fin_w.at[u, rows], (d_o, u_o)[u].at[rows])
+        else:
+            for i in (2 * n, 2 * n + 1):
+                rows = pl.ds(i * 128, 128)
+                if i < 3:
+                    qkv_w[i] = fin_b[2, rows].astype(F32).T
+                    leave(qkv_w.at[i], (q_o, k_o, v_o)[i])
+                else:
+                    fin_w[2, pl.ds(0, 128)] = fin_b[2, rows].astype(F32)
+                    leave(fin_w.at[2, pl.ds(0, 128)], o_o)
+    for copy in leaving:
+        copy.wait()
 
 
 def body(
@@ -978,7 +1033,7 @@
     others = pairs - 1
     anywhere = pl.BlockSpec(memory_space=pl.ANY)
     vmem = pl.BlockSpec(memory_space=pltpu.VMEM)
-    copies = 7 * 4 + 1 + 10 * KINDS + 8 + 4 + 5 + len(CHUNKS) * (4 + 2 * others) + 3 + others
+    copies = 7 * 4 + 1 + 7 * KINDS + 8 + 4 + 5 + len(CHUNKS) * (4 + 2 * others) + 7 + others
     square = (512, 512)
     buffers = dict(
         xin=(square, BF16),
@@ -1034,8 +1089,9 @@
         ig_s=(square, BF16),
         part=((3, 2, 2, 512, 512), BF16),
         buf_core=((3, 2, 512, 512), BF16),
-        gain_part=((5, 8, 512), F32),
-        gain_buf=((3 + others, 8, 512), F32),
+        gain_part=((1, 8, 512), F32),
+        gain_sum=((2, 8, 128), F32),
+        gain_buf=((7 + others, 8, 128), F32),
     )
     shapes = list(buffers.values())
     for _, _, rows, _, lanes, _ in CHUNKS:
@@ -1081,17 +1137,8 @@
         feedforward_norm_gain[None],
     )
 
-    def whole(shape):
-        return pl.BlockSpec(shape, lambda g: (0,) * len(shape))
-
-    def rows_block(u):
-        return pl.BlockSpec((1, 128, 512), lambda g: (u, g, 0))
-
-    tok_block = pl.BlockSpec((batch // 4, length, share), lambda g: (g, 0, 0))
-    wide_block = pl.BlockSpec((128, 512), lambda g: (g, 0))
     lo, ig, q_w, k_w, v_w, o_w, u_w, d_w, g_one, g_two = pl.pallas_call(
         widen_kernel,
-        grid=(4,),
         out_shape=(
             jax.ShapeDtypeStruct((batch, length, share), BF16),
             jax.ShapeDtypeStruct((batch, length, share), F32),
@@ -1104,29 +1151,21 @@
             jax.ShapeDtypeStruct((128,), F32),
             jax.ShapeDtypeStruct((128,), F32),
         ),
-        in_specs=[
-            tok_block,
-            tok_block,
-            rows_block(0),
-            rows_block(1),
-            rows_block(2),
-            whole((8, 128)),
+        in_specs=[anywhere] * 3 + [vmem],
+        out_specs=(anywhere,) * 8 + (vmem,) * 2,
+        scratch_shapes=[
+            pltpu.VMEM((batch, length, share), BF16),
+            pltpu.VMEM((3, 512, 512), BF16),
+            pltpu.VMEM((batch, length, share), BF16),
+            pltpu.VMEM((batch, length, share), F32),
+            pltpu.VMEM((3, 512, 512), F32),
+            pltpu.VMEM((3, 512, 128), F32),
+            pltpu.SemaphoreType.DMA((12,)),
+            pltpu.SemaphoreType.DMA((14,)),
         ],
-        out_specs=(
-            tok_block,
-            tok_block,
-            whole((512, 128)),
-            whole((512, 128)),
-            whole((512, 128)),
-            whole((128, 512)),
-            wide_block,
-            wide_block,
-            whole((128,)),
-            whole((128,)),
-        ),
         compiler_params=pltpu.CompilerParams(vmem_limit_bytes=58 * MIB),
         name="widen",
-    )(lo, ig, fin, fin, fin, gains)
+    )(lo, ig, fin, gains)
     return (lo, ig, g_one, q_w, k_w, v_w, o_w, g_two, u_w, d_w)
 
 

time: 123 us -> 113 us (0.919)
  Pallas kernels: 122 us -> 113 us
    pallas_call x1, Pallas kernels: 117 us -> 108 us  [body(): pl.pallas_call(functools.partial(layer_kernel, pairs, list(buffers)), out...]
where the time goes in v3:
time: 113 us
  Pallas kernels  113 us (100%)
    pallas_call x1, Pallas kernels, body(): pl.pallas_call(functools.partial(layer_kernel, pairs, list(buffers)), out...  108 us
    pallas_call x1, Pallas kernels, body(): pl.pallas_call(widen_kernel, out_shape=(jax.ShapeDtypeStruct((batch, leng...  4.57 us

profile of v3, /device:TPU:0, one launch (start us, length us, event | category | flops | bytes accessed | tf_op | source)
XLA Modules:
  0.0 113.2 jit_solution(7090772460740157393)
XLA Ops:
  0.6 108.0 %layer.1 = (bf16[8,256,128]{2,1,0:T(8,128)(2,1)}, bf16[8,256,128]{2,1,0:T(8,128)(2,1)}, bf16[3,512,512]{2,1,0:T(8,128)(2,1)}, f32[8,128]{1,0:T(8,128)}) custom-call(bf16[8,256,128]{2,1,0:T(8,128)(2,1)} %refs_0_.1, bf16[8,256,128]{2,1,0:T(8,128)(2,1)} %refs_1_.1, bf16[512,128]{1,0:T(8,128)(2,1)} %refs_2_.1, bf16[512,128]{1,0:T(8,128)(2,1)} %refs_3_.1, ...), custom_call_target="tpu_custom_call" | custom-call | flops 11000000512 | bytes 8388608 | tf_op jit(solution)/shard_map/layer/pallas_call | solution.py:1108
  108.6 4.6 %widen.1 = (bf16[8,256,128]{2,1,0:T(8,128)(2,1)}, f32[8,256,128]{2,1,0:T(8,128)}, f32[512,128]{1,0:T(8,128)}, f32[512,128]{1,0:T(8,128)}, f32[512,128]{1,0:T(8,1...) custom-call(bf16[8,256,128]{2,1,0:T(8,128)(2,1)} %get-tuple-element.24.lo, ...), custom_call_target="tpu_custom_call" | custom-call | tf_op jit(solution)/shard_map/widen/pallas_call | solution.py:1140

commit v4 on v3

--- a/solution.py
+++ b/solution.py
@@ -18,13 +18,13 @@
 KINDS = 4
 OWNERS = 4
 CHUNKS = (
-    (0, 0, 512, 0, 256, True),
-    (0, 0, 512, 256, 256, True),
-    (1, 0, 512, 0, 256, False),
-    (1, 0, 512, 256, 256, True),
-    (2, 384, 128, 0, 512, True),
-    (2, 0, 384, 0, 256, True),
-    (2, 0, 384, 256, 256, False),
+    (0, 0, 512, 0, 256, True, False),
+    (0, 0, 512, 256, 256, False, False),
+    (1, 0, 512, 0, 256, False, False),
+    (1, 0, 512, 256, 256, False, False),
+    (2, 384, 128, 0, 512, True, False),
+    (2, 0, 384, 0, 256, True, False),
+    (2, 0, 384, 256, 256, True, True),
 )
 COMBOS = ((0, 1, 0), (0, 1, 1), (1, 1, 0), (1, 1, 1), (1, 0, 0), (1, 0, 1), (0, 0, 1))
 
@@ -512,10 +512,11 @@
 
     class Chunk:
         def __init__(self, n):
-            self.u, self.row, self.rows, self.lane, self.lanes, self.y_first = CHUNKS[n]
+            self.u, self.row, self.rows, self.lane, self.lanes = CHUNKS[n][:5]
+            self.y_first, self.x_then_z = CHUNKS[n][5:]
             self.half = self.rows // 2
             self.piece = self.half // OWNERS
-            self.buf, self.ring_buf, self.own = chunk_refs[3 * n : 3 * n + 3]
+            self.buf, self.ring_buf, self.own, self.own_x = chunk_refs[4 * n : 4 * n + 4]
             self.cols = pl.ds(self.lane, self.lanes)
             self.devices = (ypeer, xpeer) if self.y_first else (xpeer, ypeer)
             self.ring_base = self.spread_base = None
@@ -579,8 +580,8 @@
 
             each_ring(go)
 
-        def final(self, index):
-            rows = self.rows_of(par, lax.rem(index, OWNERS) * self.piece, self.piece)
+        def final(self, index, half=par):
+            rows = self.rows_of(half, lax.rem(index, OWNERS) * self.piece, self.piece)
             return fin.at[self.u, rows, self.cols]
 
         def spread_copy(self, d):
@@ -592,6 +593,11 @@
             self.spread_base = take(pairs - 1)
             sem = local_sem.at[next(local_ids)]
             self.kept = pltpu.make_async_copy(self.own, self.final(pair), sem)
+            if self.x_then_z:
+                self.across = remote(self.own, self.own_x, xpeer)
+                self.spread_x_base = take(pairs - 1)
+                sem = local_sem.at[next(local_ids)]
+                self.kept_x = pltpu.make_async_copy(self.own_x, self.final(pair, 1 - par), sem)
 
             def total():
                 each_ring(lambda d: self.ring_copy(d)[0].wait_recv())
@@ -610,24 +616,52 @@
                     self.own[...] = value.astype(BF16)
                 else:
                     each_ring(more)
+                if self.x_then_z:
+                    self.across.start()
                 each_ring(lambda d: self.spread_copy(d).start())
                 self.kept.start()
 
             guarded(owner, total)
 
-        def back(self):
-            def arrived(d):
+        def spread_x_copy(self, d):
+            return remote(
+                self.own_x,
+                self.final(pair, 1 - par),
+                ring(d)[1],
+                self.spread_x_base + d - 1,
+            )
+
+        def arrived(self, copy_of):
+            def one(d):
                 giver = lax.rem(pair - d + pairs, pairs)
                 cond = None if pairs == OWNERS else giver < OWNERS
-                guarded(cond, self.spread_copy(d).wait_recv)
-
-            each_ring(arrived)
+                guarded(cond, copy_of(d).wait_recv)
+
+            each_ring(one)
+
+        def back(self):
+            if self.x_then_z:
+
+                def pass_on():
+                    self.across.wait_recv()
+                    each_ring(lambda d: self.spread_x_copy(d).start())
+                    self.kept_x.start()
+
+                guarded(owner, pass_on)
+                return
+            self.arrived(self.spread_copy)
             guarded(owner, self.kept.wait)
             rows = fin.at[self.u, self.rows_of(par), self.cols]
             self.last = send(rows, rows, xpeer)
 
         def end(self):
-            self.last.wait_recv()
+            if self.x_then_z:
+                self.arrived(self.spread_copy)
+                self.arrived(self.spread_x_copy)
+                guarded(owner, self.kept.wait)
+                guarded(owner, self.kept_x.wait)
+            else:
+                self.last.wait_recv()
 
         def sent(self):
             def one(d):
@@ -636,7 +670,11 @@
 
             each_ring(one)
             guarded(owner, lambda: each_ring(lambda d: self.spread_copy(d).wait_send()))
-
+            if self.x_then_z:
+                guarded(owner, self.across.wait_send)
+                guarded(owner, lambda: each_ring(lambda d: self.spread_x_copy(d).wait_send()))
+
+    lo_copies, ig_copies = [], []
     d0, d1, u0, u1, o0, a0, a1 = chunks = [Chunk(n) for n in range(len(CHUNKS))]
 
     def zero_rows(r):
@@ -679,8 +717,9 @@
     weight_last(2)
     feed(hc, hy)
     core_fed(core_f, hy)
+    weight_last(3)
+    u1.b()
     u0.b()
-    weight_last(3)
     feed_on(hc, hy)
     weight_ready(2)
     weight_ready(3)
@@ -689,14 +728,10 @@
     feed_on(1 - hc, 1 - hy)
     feed(hc, 1 - hy)
     core_fed(core_f, 1 - hy)
-    for chunk in (d0, d1):
-        chunk.a()
-        chunk.b()
+    u1.a()
+    feed_on(hc, 1 - hy)
+
     u0.a()
-    u1.a()
-    u1.b()
-    feed_on(hc, 1 - hy)
-
     gain_part[0] = jnp.zeros((8, 512), F32)
     row_512 = lax.broadcasted_iota(jnp.int32, (8, 512), 0)
 
@@ -724,7 +759,8 @@
         norm_grad, gain_two, unit_two, rstd_two, lambda r: ogs[r, :].astype(F32), sink_middle, 1
     )
 
-    lo_copies = scatter_out(lo_s, lo_out, COMBOS[4:])
+    d1.b()
+    d0.a()
     lo_own = local(lo_s.at[half256, hcol], lo_out.at[member])
     out_rows = pl.ds(384, 128)
     work_two[...] = mm(attn[...], middle_low[...], "TN")
@@ -771,6 +807,8 @@
         def _():
             for copy in backward[d]:
                 copy.start()
+
+    u1.mid()
 
     marks = jnp.where(first_lane | second_lane, 1.0, 0.0).astype(BF16)
     marks = jnp.broadcast_to(marks, (256, 128))
@@ -793,16 +831,15 @@
         val_acc[rows, cols] = mm(scores_low[i], gnum_two, "TN")
 
     loop(4, inner)
-    d0.mid()
-    u0.mid()
+    d0.b()
     core_o.wait_recv()
     add_core(2, 0, 384, 128)
     add_core(2, 1, 384, 128)
+    d0.mid()
     loop(4, lambda i: inner(4 + i))
 
-    d1.mid()
-    o0.a()
-    o0.b()
+    d1.a()
+    u1.ring()
     for d in (1, 2):
 
         @pl.when(pair + d < pairs)
@@ -813,6 +850,7 @@
     pass_on = buf_gz[0, pl.ds(4, 1), :]
     buf_gz[0] = buf_gz[0] + pass_on * buf_gz[1]
 
+    o0.a()
     def leave(i):
         b, pr, rows, cols = place(i)
         leaving = buf_gs[0, packed_rows(pr), :].astype(F32) + pass_on * buf_gs[
@@ -833,6 +871,8 @@
 
     loop(8, leave)
 
+    u0.mid()
+    lo_copies += scatter_out(lo_s, lo_out, COMBOS[4:])
     d0.ring()
     def qkv_weight(i):
         work[...] = mm(low_grads[i], normed[...], "TN")
@@ -846,17 +886,18 @@
         for jy in (1 - hy, hy)
     ]
     norm_grad[...] = mm(low_grads[0], w_qkv[0], "NT")
+    o0.b()
+    u1.spread()
     core_a[0].wait_recv()
     add_core(2, 1 - hy, 0, 384)
-    a0.a()
-    a1.a()
     core_a[1].wait_recv()
     add_core(2, hy, 0, 384)
+    a0.a()
     a0.b()
-    a1.b()
     norm_grad[...] += mm(low_grads[1], w_qkv[1], "NT")
+    u0.ring()
+    o0.mid()
     norm_grad[...] += mm(low_grads[2], w_qkv[2], "NT")
-    u1.mid()
 
     def sink_input(r, grad):
         ig_s[r, :] = grad.astype(BF16)
@@ -900,33 +941,33 @@
         each_ring(add_gain)
         gains[...] = gain_sum[1]
 
+    d0.spread()
+    a1.a()
+    ig_copies += scatter_out(ig_s, ig_out, COMBOS[4:])
+    d1.mid()
+    a0.mid()
+    u1.back()
+    ig_copies += scatter_out(ig_s, ig_out, COMBOS[:4])
+    o0.ring()
     gain_copies = gain_start()
+    ig_own = local(ig_s.at[half256, hcol], ig_out.at[member])
+    a1.mid()
+    a0.ring()
+    d0.back()
+    u0.spread()
+    o0.spread()
+    a1.b()
     d1.ring()
-    d0.spread()
-    u0.ring()
-    u1.ring()
-    o0.mid()
-    d1.spread()
-    d0.back()
-    a0.mid()
-    a1.mid()
-    o0.ring()
-    u0.spread()
-    a0.ring()
-    a1.ring()
-    lo_copies += scatter_out(lo_s, lo_out, COMBOS[:4])
-    ig_copies = scatter_out(ig_s, ig_out, COMBOS)
-    ig_own = local(ig_s.at[half256, hcol], ig_out.at[member])
-    d1.back()
-    u1.spread()
-    gain_middle(gain_copies)
-    o0.spread()
     u0.back()
     a0.spread()
+    lo_copies += scatter_out(lo_s, lo_out, COMBOS[:4])
+    a1.ring()
+    d1.spread()
+    a0.back()
     a1.spread()
-    u1.back()
+    gain_middle(gain_copies)
     o0.back()
-    a0.back()
+    d1.back()
     a1.back()
     gain_end()
 
@@ -1033,7 +1074,7 @@
     others = pairs - 1
     anywhere = pl.BlockSpec(memory_space=pl.ANY)
     vmem = pl.BlockSpec(memory_space=pltpu.VMEM)
-    copies = 7 * 4 + 1 + 7 * KINDS + 8 + 4 + 5 + len(CHUNKS) * (4 + 2 * others) + 7 + others
+    copies = 7 * 4 + 1 + 7 * KINDS + 8 + 4 + 5 + len(CHUNKS) * (4 + 3 * others) + 7 + others
     square = (512, 512)
     buffers = dict(
         xin=(square, BF16),
@@ -1094,14 +1135,15 @@
         gain_buf=((7 + others, 8, 128), F32),
     )
     shapes = list(buffers.values())
-    for _, _, rows, _, lanes, _ in CHUNKS:
+    for _, _, rows, _, lanes, _, _ in CHUNKS:
         piece = rows // 2 // OWNERS
         shapes.append(((3, rows // 2, lanes), BF16))
         shapes.append(((others, piece, lanes), BF16))
         shapes.append(((piece, lanes), BF16))
+        shapes.append(((piece, lanes), BF16))
     scratch = [pltpu.VMEM(*spec) for spec in shapes]
     scratch += [
-        pltpu.SemaphoreType.DMA((8 + 2 + len(CHUNKS),)),
+        pltpu.SemaphoreType.DMA((8 + 2 + 2 * len(CHUNKS),)),
         pltpu.SemaphoreType.DMA((copies,)),
         pltpu.SemaphoreType.DMA((copies,)),
     ]

time: 113 us -> 108 us (0.956)
  Pallas kernels: 113 us -> 107 us
    pallas_call x1, Pallas kernels: 108 us -> 102 us  [body(): pl.pallas_call(functools.partial(layer_kernel, pairs, list(buffers)), out...]
where the time goes in v4:
time: 108 us; the launch traced here: 107 us
  Pallas kernels  107 us (99%)
    pallas_call x1, Pallas kernels, body(): pl.pallas_call(functools.partial(layer_kernel, pairs, list(buffers)), out...  102 us
    pallas_call x1, Pallas kernels, body(): pl.pallas_call(widen_kernel, out_shape=(jax.ShapeDtypeStruct((batch, leng...  4.57 us

profile of v4, /device:TPU:0, one launch (start us, length us, event | category | flops | bytes accessed | tf_op | source)
XLA Modules:
  0.0 107.5 jit_solution(14547131251739651806)
XLA Ops:
  0.6 102.2 %layer.1 = (bf16[8,256,128]{2,1,0:T(8,128)(2,1)}, bf16[8,256,128]{2,1,0:T(8,128)(2,1)}, bf16[3,512,512]{2,1,0:T(8,128)(2,1)}, f32[8,128]{1,0:T(8,128)}) custom-call(bf16[8,256,128]{2,1,0:T(8,128)(2,1)} %refs_0_.1, bf16[8,256,128]{2,1,0:T(8,128)(2,1)} %refs_1_.1, bf16[512,128]{1,0:T(8,128)(2,1)} %refs_2_.1, bf16[512,128]{1,0:T(8,128)(2,1)} %refs_3_.1, ...), custom_call_target="tpu_custom_call" | custom-call | flops 11000000512 | bytes 8388608 | tf_op jit(solution)/shard_map/layer/pallas_call | solution.py:1150
  102.9 4.6 %widen.1 = (bf16[8,256,128]{2,1,0:T(8,128)(2,1)}, f32[8,256,128]{2,1,0:T(8,128)}, f32[512,128]{1,0:T(8,128)}, f32[512,128]{1,0:T(8,128)}, f32[512,128]{1,0:T(8,1...) custom-call(bf16[8,256,128]{2,1,0:T(8,128)(2,1)} %get-tuple-element.24.lo, ...), custom_call_target="tpu_custom_call" | custom-call | tf_op jit(solution)/shard_map/widen/pallas_call | solution.py:1182

commit v5 on v4

--- a/solution.py
+++ b/solution.py
@@ -18,13 +18,13 @@
 KINDS = 4
 OWNERS = 4
 CHUNKS = (
-    (0, 0, 512, 0, 256, True, False),
-    (0, 0, 512, 256, 256, False, False),
+    (0, 0, 512, 0, 256, True, True),
+    (0, 0, 512, 256, 256, True, False),
     (1, 0, 512, 0, 256, False, False),
     (1, 0, 512, 256, 256, False, False),
-    (2, 384, 128, 0, 512, True, False),
-    (2, 0, 384, 0, 256, True, False),
-    (2, 0, 384, 256, 256, True, True),
+    (2, 384, 128, 0, 512, False, False),
+    (2, 0, 384, 0, 256, False, False),
+    (2, 0, 384, 256, 256, True, False),
 )
 COMBOS = ((0, 1, 0), (0, 1, 1), (1, 1, 0), (1, 1, 1), (1, 0, 0), (1, 0, 1), (0, 0, 1))
 
@@ -34,12 +34,12 @@
     return lax.dot_general(left, right, (dims, ((), ())), preferred_element_type=F32)
 
 
-def loop(count, step):
+def loop(count, step, unroll=1):
     def run(i, carry):
         step(i)
         return carry
 
-    lax.fori_loop(0, count, run, 0)
+    lax.fori_loop(0, count, run, 0, unroll=unroll)
 
 
 def span(start, size, multiple=None):
@@ -245,7 +245,8 @@
 
     def weight_core(kind):
         own = view(kind, h)
-        wt[kind, "c"] = [send(own, own, core)]
+        wt[kind, "own"] = send(own, own, core)
+        wt[kind, "c"] = []
 
     def weight_near(kind):
         wt[kind, "y"].wait_recv()
@@ -263,30 +264,35 @@
         wt[kind, "c"].append(pass_on_weight(kind, 4 * (1 - zb), 4, core))
 
     def weight_own(kind):
-        wt[kind, "c"][0].wait_recv()
+        wt[kind, "own"].wait_recv()
 
     def weight_ready(kind):
-        for copy in wt[kind, "c"][1:]:
+        for copy in wt[kind, "c"]:
             copy.wait_recv()
 
-    for copy in own_w[0]:
-        copy.wait()
+    for copies in own_w:
+        for copy in copies:
+            copy.wait()
+    seg_copy = send(seg, seg_other, xpeer)
+    tokens_in, og_copies = [], []
     weight_y(0)
-    tokens_in = scatter_in(tok, xin)
-    seg_copy = send(seg, seg_other, xpeer)
+    tokens_in += scatter_in(tok, xin, COMBOS[0:2])
+    tokens_in += scatter_in(tok, xin, COMBOS[2:4])
+    tokens_in += scatter_in(tok, xin, COMBOS[4:])
     weight_core(0)
-    for kind in (1, 2, 3):
-        for copy in own_w[kind]:
-            copy.wait()
-        weight_y(kind)
-    for kind in (1, 2, 3):
-        weight_core(kind)
+    weight_y(1)
+    weight_y(2)
+    weight_y(3)
+    weight_core(1)
+    weight_core(2)
+    weight_core(3)
     weight_near(0)
-    og_copies = scatter_in(og_in, ogs)
+    og_copies += scatter_in(og_in, ogs, COMBOS[0:2])
+    og_copies += scatter_in(og_in, ogs, COMBOS[2:4])
+    og_copies += scatter_in(og_in, ogs, COMBOS[4:])
     for copy in tokens_in:
         copy.wait_recv()
     own_tok.wait()
-    weight_far(0)
 
     def norm_rows(source, gain, unit_ref, rstd_ref, out_ref):
         def step(r):
@@ -302,6 +308,7 @@
 
     norm_rows(lambda r: xin[r, :].astype(F32), gain_one, unit_one, rstd_one, normed)
 
+    weight_far(0)
     seg_copy.wait_recv()
     own_row = seg[pl.ds(member, 1), :]
     other_row = seg_other[pl.ds(member, 1), :]
@@ -317,7 +324,6 @@
         mask[b] = jnp.where((along == down) & (second <= first), 1.0, 0.0)
         seg_col[b] = down[:, :128]
     weight_own(0)
-
     lane = lax.broadcasted_iota(jnp.int32, (1, 128), 1)
     low_lanes = lane < 64
     spread = (
@@ -382,11 +388,14 @@
 
     forward = {}
 
-    def send_state(order, side):
-        loop(4, lambda i: own_state(i, side))
+    def make_state(order, side):
+        loop(4, lambda i: own_state(i, side), 2)
         rows = span(side * 128, 128)
         msg_s[rows, :] = (own_s[1, rows, :] + keep_mid * own_s[0, rows, :]).astype(BF16)
         msg_z[order] = jnp.where(row8 == 4, last_rows[1], own_z[1] + keep_mid * own_z[0])
+
+    def send_state(order, side):
+        rows = span(side * 128, 128)
         for d in (1, 2):
             copies = shift(
                 d,
@@ -405,12 +414,14 @@
 
     own_z[...] = jnp.zeros_like(own_z)
     project(hy)
+    make_state(0, hy)
     send_state(0, hy)
     weight_near(1)
     weight_last(0)
     weight_near(2)
     weight_ready(0)
     project(1 - hy)
+    make_state(1, 1 - hy)
     send_state(1, 1 - hy)
     weight_far(1)
     weight_near(3)
@@ -470,16 +481,15 @@
 
     receive_state(0)
     enter(0, hy)
-    loop(4, lambda i: attend(i, hy))
+    loop(4, lambda i: attend(i, hy), 2)
     weight_far(2)
     receive_state(1)
     enter(1, 1 - hy)
     weight_last(1)
-    loop(4, lambda i: attend(i, 1 - hy))
+    loop(4, lambda i: attend(i, 1 - hy), 2)
     keep_first = ready["keep_first"]
     weight_own(1)
     weight_ready(1)
-
     weight_far(3)
     work[...] = mm(attn[...], w_o[...])
 
@@ -714,24 +724,24 @@
     feed(1 - hc, hy)
     core_f = core_feed(hy)
     feed_on(1 - hc, hy)
-    weight_last(2)
     feed(hc, hy)
     core_fed(core_f, hy)
+    weight_last(2)
     weight_last(3)
-    u1.b()
     u0.b()
     feed_on(hc, hy)
     weight_ready(2)
     weight_ready(3)
+    u1.b()
     feed(1 - hc, 1 - hy)
     core_f = core_feed(1 - hy)
     feed_on(1 - hc, 1 - hy)
     feed(hc, 1 - hy)
     core_fed(core_f, 1 - hy)
-    u1.a()
+    u0.a()
+    d1.a()
     feed_on(hc, 1 - hy)
 
-    u0.a()
     gain_part[0] = jnp.zeros((8, 512), F32)
     row_512 = lax.broadcasted_iota(jnp.int32, (8, 512), 0)
 
@@ -759,7 +769,6 @@
         norm_grad, gain_two, unit_two, rstd_two, lambda r: ogs[r, :].astype(F32), sink_middle, 1
     )
 
-    d1.b()
     d0.a()
     lo_own = local(lo_s.at[half256, hcol], lo_out.at[member])
     out_rows = pl.ds(384, 128)
@@ -769,6 +778,7 @@
     core_o = core_send(part.at[2, :, 1 - hc, out_rows], buf_core.at[2, :, out_rows])
     work[...] = mm(middle_low[...], w_o[...], "NT")
 
+    u1.a()
     head_ones = jnp.where(spread, 1.0, 0.0).astype(BF16)
     head_ones = jnp.concatenate([head_ones, head_ones], axis=0)
     first_lane = lax.rem(lane, 64) == 0
@@ -795,7 +805,8 @@
         grad_s[b, packed_rows(pr), :] = pack(mm(queries.astype(BF16), gnum, "TN"))
         grad_z[b, pl.ds(pr, 1), :] = jnp.sum(queries * gden, axis=0, keepdims=True)
 
-    loop(8, outer)
+    loop(8, outer, 2)
+    lo_copies += scatter_out(lo_s, lo_out, COMBOS[4:])
     msg_gs[...] = (grad_s[0] + keep_first * grad_s[1]).astype(BF16)
     msg_gz[...] = jnp.where(row8 == 4, keep_first * keep_mid, grad_z[0] + keep_first * grad_z[1])
     backward = {}
@@ -808,7 +819,8 @@
             for copy in backward[d]:
                 copy.start()
 
-    u1.mid()
+    d1.mid()
+    u0.mid()
 
     marks = jnp.where(first_lane | second_lane, 1.0, 0.0).astype(BF16)
     marks = jnp.broadcast_to(marks, (256, 128))
@@ -830,16 +842,19 @@
         key_acc[rows, cols] = mm(gsc, two(q), "TN")
         val_acc[rows, cols] = mm(scores_low[i], gnum_two, "TN")
 
-    loop(4, inner)
-    d0.b()
+    loop(4, inner, 2)
     core_o.wait_recv()
     add_core(2, 0, 384, 128)
     add_core(2, 1, 384, 128)
+    u1.mid()
+    d0.b()
+    d1.b()
+    loop(4, lambda i: inner(4 + i), 2)
+
+    u0.ring()
+    o0.a()
     d0.mid()
-    loop(4, lambda i: inner(4 + i))
-
-    d1.a()
-    u1.ring()
+    o0.b()
     for d in (1, 2):
 
         @pl.when(pair + d < pairs)
@@ -850,7 +865,6 @@
     pass_on = buf_gz[0, pl.ds(4, 1), :]
     buf_gz[0] = buf_gz[0] + pass_on * buf_gz[1]
 
-    o0.a()
     def leave(i):
         b, pr, rows, cols = place(i)
         leaving = buf_gs[0, packed_rows(pr), :].astype(F32) + pass_on * buf_gs[
@@ -869,11 +883,9 @@
         vgrad = val_acc[rows, cols] + jnp.where(tail, mm(k, square), 0.0)
         low_grads[2, rows, cols] = vgrad.astype(BF16)
 
-    loop(8, leave)
-
-    u0.mid()
-    lo_copies += scatter_out(lo_s, lo_out, COMBOS[4:])
-    d0.ring()
+    loop(8, leave, 2)
+
+    u1.ring()
     def qkv_weight(i):
         work[...] = mm(low_grads[i], normed[...], "TN")
         for j in range(4):
@@ -886,18 +898,22 @@
         for jy in (1 - hy, hy)
     ]
     norm_grad[...] = mm(low_grads[0], w_qkv[0], "NT")
-    o0.b()
-    u1.spread()
     core_a[0].wait_recv()
     add_core(2, 1 - hy, 0, 384)
     core_a[1].wait_recv()
     add_core(2, hy, 0, 384)
+    u0.spread()
     a0.a()
+    a1.a()
+    o0.mid()
+    d1.ring()
     a0.b()
     norm_grad[...] += mm(low_grads[1], w_qkv[1], "NT")
-    u0.ring()
-    o0.mid()
+    a1.mid()
+    u1.spread()
     norm_grad[...] += mm(low_grads[2], w_qkv[2], "NT")
+    u0.back()
+    a1.b()
 
     def sink_input(r, grad):
         ig_s[r, :] = grad.astype(BF16)
@@ -941,34 +957,28 @@
         each_ring(add_gain)
         gains[...] = gain_sum[1]
 
-    d0.spread()
-    a1.a()
+    o0.ring()
+    a0.mid()
+    ig_copies += scatter_out(ig_s, ig_out, COMBOS[:4])
+    d1.spread()
+    u1.back()
     ig_copies += scatter_out(ig_s, ig_out, COMBOS[4:])
-    d1.mid()
-    a0.mid()
-    u1.back()
-    ig_copies += scatter_out(ig_s, ig_out, COMBOS[:4])
-    o0.ring()
+    a1.ring()
+    o0.spread()
     gain_copies = gain_start()
     ig_own = local(ig_s.at[half256, hcol], ig_out.at[member])
-    a1.mid()
     a0.ring()
+    d1.back()
+    d0.ring()
+    a1.spread()
+    a0.spread()
+    o0.back()
+    gain_middle(gain_copies)
+    d0.spread()
+    lo_copies += scatter_out(lo_s, lo_out, COMBOS[:4])
+    a1.back()
     d0.back()
-    u0.spread()
-    o0.spread()
-    a1.b()
-    d1.ring()
-    u0.back()
-    a0.spread()
-    lo_copies += scatter_out(lo_s, lo_out, COMBOS[:4])
-    a1.ring()
-    d1.spread()
     a0.back()
-    a1.spread()
-    gain_middle(gain_copies)
-    o0.back()
-    d1.back()
-    a1.back()
     gain_end()
 
     for chunk in chunks:
@@ -998,26 +1008,23 @@
 
 def widen_kernel(lo, ig, fin, gains, *refs):
     lo_o, ig_o, q_o, k_o, v_o, o_o, u_o, d_o, g_o, f_o = refs[:10]
-    ig_b, fin_b, lo_b, ig_w, fin_w, qkv_w, sem_in, sem_out = refs[10:]
-    parts = []
-    for u in (0, 1, 2):
+    ig_b, fin_b, lo_b, gains_b, ig_w, fin_w, qkv_w, g_w, f_w, sem_in, sem_out = refs[10:]
+    parts = [(fin.at[2], fin_b.at[2], 2, 0)]
+    for u in (0, 1):
         for half in range(2):
             rows = pl.ds(half * 256, 256)
             parts.append((fin.at[u, rows], fin_b.at[u, rows], u, half))
-    for quarter in range(4):
-        rows = pl.ds(quarter * 2, 2)
-        parts.append((ig.at[rows], ig_b.at[rows], 3, quarter))
     for half in range(2):
         rows = pl.ds(half * 4, 4)
-        parts.append((lo.at[rows], lo_b.at[rows], 4, half))
+        parts.append((ig.at[rows], ig_b.at[rows], 3, half))
+    parts.append((lo, lo_b, 4, 0))
+    parts.append((gains, gains_b, 5, 0))
     arriving = [
         pltpu.make_async_copy(source, into, sem_in.at[n])
         for n, (source, into, _, _) in enumerate(parts)
     ]
     for copy in arriving:
         copy.start()
-    g_o[...] = gains[0]
-    f_o[...] = gains[1]
     leaving = []
 
     def leave(source, out):
@@ -1027,11 +1034,15 @@
 
     for copy, (_, _, u, n) in zip(arriving, parts, strict=True):
         copy.wait()
-        if u == 4:
+        if u == 5:
+            g_w[...] = gains_b[0]
+            f_w[...] = gains_b[1]
+            leave(g_w, g_o)
+            leave(f_w, f_o)
+        elif u == 4:
+            leave(lo_b, lo_o)
+        elif u == 3:
             rows = pl.ds(n * 4, 4)
-            leave(lo_b.at[rows], lo_o.at[rows])
-        elif u == 3:
-            rows = pl.ds(n * 2, 2)
             ig_w[rows] = ig_b[rows].astype(F32)
             leave(ig_w.at[rows], ig_o.at[rows])
         elif u < 2:
@@ -1039,14 +1050,11 @@
             fin_w[u, rows] = fin_b[u, rows].astype(F32)
             leave(fin_w.at[u, rows], (d_o, u_o)[u].at[rows])
         else:
-            for i in (2 * n, 2 * n + 1):
-                rows = pl.ds(i * 128, 128)
-                if i < 3:
-                    qkv_w[i] = fin_b[2, rows].astype(F32).T
-                    leave(qkv_w.at[i], (q_o, k_o, v_o)[i])
-                else:
-                    fin_w[2, pl.ds(0, 128)] = fin_b[2, rows].astype(F32)
-                    leave(fin_w.at[2, pl.ds(0, 128)], o_o)
+            for i, out in enumerate((q_o, k_o, v_o)):
+                qkv_w[i] = fin_b[2, pl.ds(i * 128, 128)].astype(F32).T
+                leave(qkv_w.at[i], out)
+            fin_w[2, pl.ds(0, 128)] = fin_b[2, pl.ds(384, 128)].astype(F32)
+            leave(fin_w.at[2, pl.ds(0, 128)], o_o)
     for copy in leaving:
         copy.wait()
 
@@ -1074,7 +1082,9 @@
     others = pairs - 1
     anywhere = pl.BlockSpec(memory_space=pl.ANY)
     vmem = pl.BlockSpec(memory_space=pltpu.VMEM)
-    copies = 7 * 4 + 1 + 7 * KINDS + 8 + 4 + 5 + len(CHUNKS) * (4 + 3 * others) + 7 + others
+    passed = sum(chunk[6] for chunk in CHUNKS)
+    copies = 7 * 4 + 1 + 7 * KINDS + 8 + 4 + 5 + len(CHUNKS) * (3 + 2 * others)
+    copies += passed * (1 + others) + (len(CHUNKS) - passed) + 7 + others
     square = (512, 512)
     buffers = dict(
         xin=(square, BF16),
@@ -1143,7 +1153,7 @@
         shapes.append(((piece, lanes), BF16))
     scratch = [pltpu.VMEM(*spec) for spec in shapes]
     scratch += [
-        pltpu.SemaphoreType.DMA((8 + 2 + 2 * len(CHUNKS),)),
+        pltpu.SemaphoreType.DMA((8 + 2 + len(CHUNKS) + passed,)),
         pltpu.SemaphoreType.DMA((copies,)),
         pltpu.SemaphoreType.DMA((copies,)),
     ]
@@ -1193,17 +1203,20 @@
             jax.ShapeDtypeStruct((128,), F32),
             jax.ShapeDtypeStruct((128,), F32),
         ),
-        in_specs=[anywhere] * 3 + [vmem],
-        out_specs=(anywhere,) * 8 + (vmem,) * 2,
+        in_specs=[anywhere] * 4,
+        out_specs=(anywhere,) * 10,
         scratch_shapes=[
             pltpu.VMEM((batch, length, share), BF16),
             pltpu.VMEM((3, 512, 512), BF16),
             pltpu.VMEM((batch, length, share), BF16),
+            pltpu.VMEM((8, 128), F32),
             pltpu.VMEM((batch, length, share), F32),
             pltpu.VMEM((3, 512, 512), F32),
             pltpu.VMEM((3, 512, 128), F32),
-            pltpu.SemaphoreType.DMA((12,)),
-            pltpu.SemaphoreType.DMA((14,)),
+            pltpu.VMEM((128,), F32),
+            pltpu.VMEM((128,), F32),
+            pltpu.SemaphoreType.DMA((9,)),
+            pltpu.SemaphoreType.DMA((13,)),
         ],
         compiler_params=pltpu.CompilerParams(vmem_limit_bytes=58 * MIB),
         name="widen",

time: 108 us -> 103 us (0.954)
  Pallas kernels: 107 us -> 102 us
    pallas_call x1, Pallas kernels: 102 us -> 98.5 us  [body(): pl.pallas_call(functools.partial(layer_kernel, pairs, list(buffers)), out...]
where the time goes in v5:
time: 103 us
  Pallas kernels  102 us (99%)
    pallas_call x1, Pallas kernels, body(): pl.pallas_call(functools.partial(layer_kernel, pairs, list(buffers)), out...  98.5 us
    pallas_call x1, Pallas kernels, body(): pl.pallas_call(widen_kernel, out_shape=(jax.ShapeDtypeStruct((batch, leng...  3.52 us

profile of v5, /device:TPU:0, one launch (start us, length us, event | category | flops | bytes accessed | tf_op | source)
XLA Modules:
  0.0 102.8 jit_solution(7182483198469101484)
XLA Ops:
  0.6 98.5 %layer.1 = (bf16[8,256,128]{2,1,0:T(8,128)(2,1)}, bf16[8,256,128]{2,1,0:T(8,128)(2,1)}, bf16[3,512,512]{2,1,0:T(8,128)(2,1)}, f32[8,128]{1,0:T(8,128)}) custom-call(bf16[8,256,128]{2,1,0:T(8,128)(2,1)} %refs_0_.1, bf16[8,256,128]{2,1,0:T(8,128)(2,1)} %refs_1_.1, bf16[512,128]{1,0:T(8,128)(2,1)} %refs_2_.1, bf16[512,128]{1,0:T(8,128)(2,1)} %refs_3_.1, ...), custom_call_target="tpu_custom_call" | custom-call | flops 11000000512 | bytes 8388608 | tf_op jit(solution)/shard_map/layer/pallas_call | solution.py:1160
  99.1 3.5 %widen.1 = (bf16[8,256,128]{2,1,0:T(8,128)(2,1)}, f32[8,256,128]{2,1,0:T(8,128)}, f32[512,128]{1,0:T(8,128)}, f32[512,128]{1,0:T(8,128)}, f32[512,128]{1,0:T(8,1...) custom-call(bf16[8,256,128]{2,1,0:T(8,128)(2,1)} %get-tuple-element.24.lo, ...), custom_call_target="tpu_custom_call" | custom-call | tf_op jit(solution)/shard_map/widen/pallas_call | solution.py:1192

commit v6 on v5

--- a/solution.py
+++ b/solution.py
@@ -189,31 +189,32 @@
     )
     pl.semaphore_wait(barrier, len(COMBOS) + pairs - 1)
 
-    def scatter_in(src, dst, combos=COMBOS):
-        copies = []
-        for d in combos:
-            par_to, y_to, c_to = peer(*d)
-            copies.append(
-                send(
-                    src.at[par_to * 4 + 2 * y_to + c_to],
-                    dst.at[half256, hcol],
-                    address(par_to, y_to, c_to),
-                )
-            )
-        return copies
-
-    def scatter_out(src, dst, combos):
-        copies = []
-        for d in combos:
-            par_to, y_to, c_to = peer(*d)
-            copies.append(
-                send(
-                    src.at[span(par_to * 256, 256), at128(2 * y_to + c_to)],
-                    dst.at[member],
-                    address(par_to, y_to, c_to),
-                )
-            )
-        return copies
+    class Exchange:
+        def __init__(self, src, dst, seven):
+            self.src, self.dst, self.seven, self.i = src, dst, seven, take()
+
+        def go(self, combos):
+            for d in combos:
+                par_to, y_to, c_to = peer(*d)
+                to = address(par_to, y_to, c_to)
+                remote(*self.views(par_to, y_to, c_to), to, self.i).start()
+
+        def all(self):
+            return remote(self.seven, self.seven, core, self.i)
+
+    class Inward(Exchange):
+        def views(self, par_to, y_to, c_to):
+            return self.src.at[par_to * 4 + 2 * y_to + c_to], self.dst.at[half256, hcol]
+
+    class Outward(Exchange):
+        def views(self, par_to, y_to, c_to):
+            rows, cols = span(par_to * 256, 256), at128(2 * y_to + c_to)
+            return self.src.at[rows, cols], self.dst.at[member]
+
+    tok_move = Inward(tok, xin, xin.at[pl.ds(0, 448)])
+    og_move = Inward(og_in, ogs, ogs.at[pl.ds(0, 448)])
+    lo_move = Outward(lo_s, lo_out, lo_s.at[pl.ds(0, 448)])
+    ig_move = Outward(ig_s, ig_out, ig_s.at[pl.ds(0, 448)])
 
     across = 2 * (1 - hy) + hc
     quarter = par + 2 * zb
@@ -274,11 +275,10 @@
         for copy in copies:
             copy.wait()
     seg_copy = send(seg, seg_other, xpeer)
-    tokens_in, og_copies = [], []
     weight_y(0)
-    tokens_in += scatter_in(tok, xin, COMBOS[0:2])
-    tokens_in += scatter_in(tok, xin, COMBOS[2:4])
-    tokens_in += scatter_in(tok, xin, COMBOS[4:])
+    tok_move.go(COMBOS[0:2])
+    tok_move.go(COMBOS[2:4])
+    tok_move.go(COMBOS[4:])
     weight_core(0)
     weight_y(1)
     weight_y(2)
@@ -287,11 +287,10 @@
     weight_core(2)
     weight_core(3)
     weight_near(0)
-    og_copies += scatter_in(og_in, ogs, COMBOS[0:2])
-    og_copies += scatter_in(og_in, ogs, COMBOS[2:4])
-    og_copies += scatter_in(og_in, ogs, COMBOS[4:])
-    for copy in tokens_in:
-        copy.wait_recv()
+    og_move.go(COMBOS[0:2])
+    og_move.go(COMBOS[2:4])
+    og_move.go(COMBOS[4:])
+    tok_move.all().wait_recv()
     own_tok.wait()
 
     def norm_rows(source, gain, unit_ref, rstd_ref, out_ref):
@@ -500,8 +499,7 @@
     norm_rows(
         lambda r: middle[r, :].astype(BF16).astype(F32), gain_two, unit_two, rstd_two, normed_two
     )
-    for copy in og_copies:
-        copy.wait_recv()
+    og_move.all().wait_recv()
     own_og.wait()
     weight_own(2)
     weight_own(3)
@@ -519,6 +517,8 @@
         loop(rows // 64, step)
 
     owner = None if pairs == OWNERS else pair < OWNERS
+    apart = 0 if pairs == OWNERS else 1
+    in_ring = pairs - 1 if apart else 1
 
     class Chunk:
         def __init__(self, n):
@@ -565,7 +565,7 @@
                 part.at[self.u, hy, hc, rows, self.cols],
                 self.ring_buf.at[d - 1],
                 device,
-                self.ring_base + d - 1,
+                self.ring_base + apart * (d - 1),
             )
             return copy, None if pairs == OWNERS else to < OWNERS
 
@@ -582,7 +582,7 @@
                 ).astype(BF16)
 
             loop(OWNERS, step)
-            self.ring_base = take(pairs - 1)
+            self.ring_base = take(in_ring)
 
             def go(d):
                 copy, cond = self.ring_copy(d)
@@ -596,21 +596,21 @@
 
         def spread_copy(self, d):
             return remote(
-                self.own, self.final(pair), ring(d)[1], self.spread_base + d - 1
+                self.own, self.final(pair), ring(d)[1], self.spread_base + apart * (d - 1)
             )
 
         def spread(self):
-            self.spread_base = take(pairs - 1)
+            self.spread_base = take(in_ring)
             sem = local_sem.at[next(local_ids)]
             self.kept = pltpu.make_async_copy(self.own, self.final(pair), sem)
             if self.x_then_z:
                 self.across = remote(self.own, self.own_x, xpeer)
-                self.spread_x_base = take(pairs - 1)
+                self.spread_x_base = take(in_ring)
                 sem = local_sem.at[next(local_ids)]
                 self.kept_x = pltpu.make_async_copy(self.own_x, self.final(pair, 1 - par), sem)
 
             def total():
-                each_ring(lambda d: self.ring_copy(d)[0].wait_recv())
+                self.each(self.ring_base, lambda d: self.ring_copy(d)[0].wait_recv(), True)
                 rows = self.rows_of(par, lax.rem(pair, OWNERS) * self.piece, self.piece)
                 self.own[...] = part[self.u, hy, hc, rows, self.cols]
 
@@ -638,16 +638,22 @@
                 self.own_x,
                 self.final(pair, 1 - par),
                 ring(d)[1],
-                self.spread_x_base + d - 1,
+                self.spread_x_base + apart * (d - 1),
             )
 
-        def arrived(self, copy_of):
+        def each(self, base, act, arriving):
+            if apart:
+                each_ring(act)
+                return
+            together = remote(self.ring_buf, self.ring_buf, xpeer, base)
+            (together.wait_recv if arriving else together.wait_send)()
+
+        def arrived(self, base, copy_of):
             def one(d):
                 giver = lax.rem(pair - d + pairs, pairs)
-                cond = None if pairs == OWNERS else giver < OWNERS
-                guarded(cond, copy_of(d).wait_recv)
-
-            each_ring(one)
+                guarded(giver < OWNERS, copy_of(d).wait_recv)
+
+            self.each(base, one, True)
 
         def back(self):
             if self.x_then_z:
@@ -659,15 +665,15 @@
 
                 guarded(owner, pass_on)
                 return
-            self.arrived(self.spread_copy)
+            self.arrived(self.spread_base, self.spread_copy)
             guarded(owner, self.kept.wait)
             rows = fin.at[self.u, self.rows_of(par), self.cols]
             self.last = send(rows, rows, xpeer)
 
         def end(self):
             if self.x_then_z:
-                self.arrived(self.spread_copy)
-                self.arrived(self.spread_x_copy)
+                self.arrived(self.spread_base, self.spread_copy)
+                self.arrived(self.spread_x_base, self.spread_x_copy)
                 guarded(owner, self.kept.wait)
                 guarded(owner, self.kept_x.wait)
             else:
@@ -678,13 +684,17 @@
                 copy, cond = self.ring_copy(d)
                 guarded(cond, copy.wait_send)
 
-            each_ring(one)
-            guarded(owner, lambda: each_ring(lambda d: self.spread_copy(d).wait_send()))
-            if self.x_then_z:
-                guarded(owner, self.across.wait_send)
-                guarded(owner, lambda: each_ring(lambda d: self.spread_x_copy(d).wait_send()))
-
-    lo_copies, ig_copies = [], []
+            def spread_sent():
+                self.each(self.spread_base, lambda d: self.spread_copy(d).wait_send(), False)
+                if self.x_then_z:
+                    self.across.wait_send()
+                    self.each(
+                        self.spread_x_base, lambda d: self.spread_x_copy(d).wait_send(), False
+                    )
+
+            self.each(self.ring_base, one, False)
+            guarded(owner, spread_sent)
+
     d0, d1, u0, u1, o0, a0, a1 = chunks = [Chunk(n) for n in range(len(CHUNKS))]
 
     def zero_rows(r):
@@ -806,7 +816,7 @@
         grad_z[b, pl.ds(pr, 1), :] = jnp.sum(queries * gden, axis=0, keepdims=True)
 
     loop(8, outer, 2)
-    lo_copies += scatter_out(lo_s, lo_out, COMBOS[4:])
+    lo_move.go(COMBOS[4:])
     msg_gs[...] = (grad_s[0] + keep_first * grad_s[1]).astype(BF16)
     msg_gz[...] = jnp.where(row8 == 4, keep_first * keep_mid, grad_z[0] + keep_first * grad_z[1])
     backward = {}
@@ -959,10 +969,10 @@
 
     o0.ring()
     a0.mid()
-    ig_copies += scatter_out(ig_s, ig_out, COMBOS[:4])
+    ig_move.go(COMBOS[:4])
     d1.spread()
     u1.back()
-    ig_copies += scatter_out(ig_s, ig_out, COMBOS[4:])
+    ig_move.go(COMBOS[4:])
     a1.ring()
     o0.spread()
     gain_copies = gain_start()
@@ -975,7 +985,7 @@
     o0.back()
     gain_middle(gain_copies)
     d0.spread()
-    lo_copies += scatter_out(lo_s, lo_out, COMBOS[:4])
+    lo_move.go(COMBOS[:4])
     a1.back()
     d0.back()
     a0.back()
@@ -983,12 +993,14 @@
 
     for chunk in chunks:
         chunk.end()
-    for copy in lo_copies + ig_copies:
-        copy.wait_recv()
+    lo_move.all().wait_recv()
+    ig_move.all().wait_recv()
     lo_own.wait()
     ig_own.wait()
     for copy in sends:
         copy.wait_send()
+    for move in (tok_move, og_move, lo_move, ig_move):
+        move.all().wait_send()
     for chunk in chunks:
         chunk.sent()
     each_ring(lambda d: gain_copy(d).wait_send())
@@ -1080,11 +1092,12 @@
     assert (width, share, head_cols, units) == (512, 128, 128, 512)
     assert pairs >= OWNERS and pairs % 2 == 0
     others = pairs - 1
+    in_ring = 1 if pairs == OWNERS else others
     anywhere = pl.BlockSpec(memory_space=pl.ANY)
     vmem = pl.BlockSpec(memory_space=pltpu.VMEM)
     passed = sum(chunk[6] for chunk in CHUNKS)
-    copies = 7 * 4 + 1 + 7 * KINDS + 8 + 4 + 5 + len(CHUNKS) * (3 + 2 * others)
-    copies += passed * (1 + others) + (len(CHUNKS) - passed) + 7 + others
+    copies = 4 + 1 + 7 * KINDS + 8 + 4 + 5 + len(CHUNKS) * (3 + 2 * in_ring)
+    copies += passed * (1 + in_ring) + (len(CHUNKS) - passed) + 7 + others
     square = (512, 512)
     buffers = dict(
         xin=(square, BF16),

time: 103 us -> 102 us (level)
    pallas_call x1, Pallas kernels: 98.5 us -> 97.4 us  [body(): pl.pallas_call(functools.partial(layer_kernel, pairs, list(buffers)), out...]
where the time goes in v6:
time: 102 us
  Pallas kernels  101 us (99%)
    pallas_call x1, Pallas kernels, body(): pl.pallas_call(functools.partial(layer_kernel, pairs, list(buffers)), out...  97.4 us
    pallas_call x1, Pallas kernels, body(): pl.pallas_call(widen_kernel, out_shape=(jax.ShapeDtypeStruct((batch, leng...  3.52 us

profile of v6, /device:TPU:0, one launch (start us, length us, event | category | flops | bytes accessed | tf_op | source)
XLA Modules:
  0.0 101.7 jit_solution(4055686983018873897)
XLA Ops:
  0.6 97.4 %layer.1 = (bf16[8,256,128]{2,1,0:T(8,128)(2,1)}, bf16[8,256,128]{2,1,0:T(8,128)(2,1)}, bf16[3,512,512]{2,1,0:T(8,128)(2,1)}, f32[8,128]{1,0:T(8,128)}) custom-call(bf16[8,256,128]{2,1,0:T(8,128)(2,1)} %refs_0_.1, bf16[8,256,128]{2,1,0:T(8,128)(2,1)} %refs_1_.1, bf16[512,128]{1,0:T(8,128)(2,1)} %refs_2_.1, bf16[512,128]{1,0:T(8,128)(2,1)} %refs_3_.1, ...), custom_call_target="tpu_custom_call" | custom-call | flops 11000000512 | bytes 8388608 | tf_op jit(solution)/shard_map/layer/pallas_call | solution.py:1173
  98.0 3.5 %widen.1 = (bf16[8,256,128]{2,1,0:T(8,128)(2,1)}, f32[8,256,128]{2,1,0:T(8,128)}, f32[512,128]{1,0:T(8,128)}, f32[512,128]{1,0:T(8,128)}, f32[512,128]{1,0:T(8,1...) custom-call(bf16[8,256,128]{2,1,0:T(8,128)(2,1)} %get-tuple-element.24.lo, ...), custom_call_target="tpu_custom_call" | custom-call | tf_op jit(solution)/shard_map/widen/pallas_call | solution.py:1205
